TPU v7x, 256 devices: a whole 4x4x8 slice. The times are simulated.
256 devices in a mesh: rep: 32 (over z_hi, x, core), fsdp: 8 (over z_lo, y).
Axes of the slice: x: 4, y: 4, z: 8 (z_hi: 4, z_lo: 2; z = z_hi * 2 + z_lo), core: 2. Of those that a mesh axis runs over, the one named last changes fastest.
Arguments:
- activations: bfloat16 [131072, 4096], P(('rep', 'fsdp')), may hold values from -6 to 6
- target: bfloat16 [131072, 512], P(('rep', 'fsdp')), may hold values from -6 to 6
- params: float32 [32, 4096, 512], P('rep', 'fsdp'), may hold values from -6 to 6
- momentum: float32 [32, 4096, 512], P('rep', 'fsdp'), may hold values from -6 to 6
- outer_params: float32 [4096, 512], P('fsdp'), may hold values from -6 to 6
- outer_momentum: float32 [4096, 512], P('fsdp'), may hold values from -6 to 6
- pending: float32 [1024, 512], P('fsdp'), may hold values from -6 to 6
- plan: int32 [4], replicated, may hold values from 0 to 3, each once
Outputs:
- new_params: float32 [32, 4096, 512], P('rep', 'fsdp')
- new_momentum: float32 [32, 4096, 512], P('rep', 'fsdp')
- grad_input: bfloat16 [131072, 4096], P(('rep', 'fsdp'))
- new_outer: float32 [4096, 512], P('fsdp')
- new_outer_momentum: float32 [4096, 512], P('fsdp')
- new_pending: float32 [1024, 512], P('fsdp')
Inputs may be any that keep to these rules, and one draw needn't show every extreme that they name: plan lists the 4 fragments in the order in which this round synchronizes them, each once.
All inputs are finite; a program needn't handle non-finite values.
Results may differ from a plain program's by a relative error of at most 0.018.
Values may be sent and summed in bfloat16 or wider, within the bound.
No kernel may reach another device: no remote copies, remote signals or barrier semaphores. Data moves between devices by JAX's collectives and lax.ppermute only.
A program may use at most 128 MiB of HBM per device.

v0:
```python
import jax
import jax.numpy as jnp
from jax import lax
from jax.sharding import PartitionSpec as P

DW = 4096
NFRAG = 4


INNER_RATE = 0.05
INNER_BETA = 0.9
OUTER_RATE = 0.7
OUTER_BETA = 0.9
MIX_SHARE = 0.5


def local_fragment(matrix, frag_index):
    shaped = matrix.reshape(NFRAG, -1, matrix.shape[1])
    return lax.dynamic_index_in_dim(shaped, frag_index, 0, keepdims=False)


def local_replace(matrix, frag_index, new_rows):
    shaped = matrix.reshape(NFRAG, -1, matrix.shape[1])
    updated = lax.dynamic_update_slice_in_dim(shaped, new_rows[None], frag_index, 0)
    return updated.reshape(matrix.shape)


def make_cotangent(values, target):
    return (values - target.astype(jnp.float32)).astype(jnp.bfloat16)


def body(activations, target, params, momentum, outer_params, outer_momentum, pending, plan):
    multiplier = DW ** (-0.5)
    weights = params[0]
    moment = momentum[0]
    weights16 = weights.astype(jnp.bfloat16)
    gathered = lax.all_gather(weights16, "fsdp", axis=0, tiled=True)
    values = jnp.dot(activations, gathered, preferred_element_type=jnp.float32) * multiplier
    cotangent = make_cotangent(values, target)
    product = lax.dot_general(
        cotangent, gathered, (((1,), (1,)), ((), ())), preferred_element_type=jnp.float32
    )
    grad_input = (product * multiplier).astype(jnp.bfloat16)
    gradient = (
        lax.psum_scatter(
            lax.dot_general(
                activations, cotangent, (((0,), (0,)), ((), ())), preferred_element_type=jnp.float32
            ).astype(jnp.bfloat16),
            "fsdp",
            scatter_dimension=0,
            tiled=True,
        ).astype(jnp.float32)
        * multiplier
    )
    new_moment = INNER_BETA * moment + gradient
    stepped = weights - INNER_RATE * new_moment
    current = plan[2]
    arrived = plan[0]
    pseudo_grad = local_fragment(outer_params, current) - local_fragment(weights, current)
    new_pending = lax.psum(pseudo_grad.astype(jnp.bfloat16), "rep").astype(
        jnp.float32
    ) / lax.axis_size("rep")
    moment_late = OUTER_BETA * local_fragment(outer_momentum, arrived) + pending
    outer_late = local_fragment(outer_params, arrived) - OUTER_RATE * (
        pending + OUTER_BETA * moment_late
    )
    new_outer_momentum = local_replace(outer_momentum, arrived, moment_late)
    new_outer = local_replace(outer_params, arrived, outer_late)
    merged = local_replace(
        stepped, arrived, MIX_SHARE * local_fragment(stepped, arrived) + MIX_SHARE * outer_late
    )
    return (merged[None], new_moment[None], grad_input, new_outer, new_outer_momentum, new_pending)


def solution(mesh):
    placed = (
        P(("rep", "fsdp"), None),
        P(("rep", "fsdp"), None),
        P("rep", "fsdp", None),
        P("rep", "fsdp", None),
        P("fsdp", None),
        P("fsdp", None),
        P("fsdp", None),
        P(),
    )
    return jax.shard_map(
        body,
        mesh=mesh,
        in_specs=placed,
        out_specs=(
            P("rep", "fsdp", None),
            P("rep", "fsdp", None),
            P(("rep", "fsdp"), None),
            P("fsdp", None),
            P("fsdp", None),
            P("fsdp", None),
        ),
        check_vma=False,
    )
```

profile of v0, /device:TPU:24, one launch (start us, length us, event | category | flops | bytes accessed | tf_op | source)
XLA Modules:
  0.0 408.1 jit_solution(11455606257852959745)
XLA Ops:
  7.2 0.0 all-gather.2.cloned.1.call-start
  7.2 1.3 copy.22
  8.5 1.2 copy.23
  9.8 0.9 bitcast_convert_fusion
  10.6 0.0 all-gather.2.cloned.1.call-update
  10.6 0.0 reduce-scatter.2.cloned.1.call-start
  10.7 55.8 %all-gather.2.cloned.1.call-done = bf16[4096,512]{1,0:T(8,128)(2,1)} async-done(((bf16[512,512]{1,0:T(8,128)(2,1)}), bf16[4096,512]{1,0:T(8,128)(2,1)}) %all-gather.2.cloned.1.call-update) | async-done | bytes 4194320 | tf_op jit(solution)/shard_map/all_gather | solution.py:37
  66.5 6.0 %fusion.2 = bf16[512,512]{1,0:T(8,128)(2,1)S(1)} fusion(bf16[512,4096]{1,0:T(8,128)(2,1)} %param.8, bf16[4096,512]{1,0:T(8,128)(2,1)} %all-gather.2.cloned.1.call-done, bf16[512,512]{1,0:T(8,128)(2,1)} %param.9), kind=kOutput, calls=%fused_computation.5 | convolution fusion | flops 2148532224 | bytes 9437184 | tf_op jit(solution)/shard_map/dot_general | solution.py:38
  72.4 0.8 copy-done.8
  73.2 4.4 %fusion = bf16[4096,512]{1,0:T(8,128)(2,1)} fusion(bf16[512,512]{1,0:T(8,128)(2,1)S(1)} %fusion.2, bf16[512,4096]{1,0:T(8,128)(2,1)S(1)} %copy-done.7), kind=kOutput, calls=%fused_computation.2 | convolution fusion | flops 2149580800 | bytes 8912896 | tf_op jit(solution)/shard_map/dot_general | solution.py:46
  77.7 0.0 reduce-scatter.2.cloned.1.call-update
  77.7 0.0 all-reduce.2.cloned.1.call-start
  77.8 0.6 copy-done.6
  78.3 0.6 fusion.6
  82.8 0.7 bitcast_add_fusion.1
  83.6 48.8 %reduce-scatter.2.cloned.1.call-done = bf16[512,512]{1,0:T(8,128)(2,1)} async-done(((bf16[4096,512]{1,0:T(8,128)(2,1)}), bf16[512,512]{1,0:T(8,128)(2,1)}) %reduce-scatter.2.cloned.1.call-update) | async-done | bytes 524304 | tf_op jit(solution)/shard_map/reduce_scatter | solution.py:45
  132.3 2.7 fusion.3
  135.0 0.1 bitcast_dynamic-update-slice_fusion.2
  135.2 0.8 fusion.5
  136.0 0.2 copy-done.3
  136.2 0.0 all-reduce.2.cloned.1.call-update
  136.2 7.1 %multiply_convert_fusion = bf16[512,4096]{1,0:T(8,128)(2,1)} fusion(bf16[512,512]{1,0:T(8,128)(2,1)} %copy-done.8, bf16[4096,512]{1,0:T(8,128)(2,1)} %all-gather.2.cloned.1.call-done), kind=kOutput, calls=%fused_computation | convolution fusion | flops 2151677952 | bytes 8912896 | tf_op jit(solution)/shard_map/dot_general | solution.py:40
  143.3 256.6 %all-reduce.2.cloned.1.call-done = bf16[128,512]{1,0:T(8,128)(2,1)} async-done(((bf16[128,512]{1,0:T(8,128)(2,1)}), bf16[128,512]{1,0:T(8,128)(2,1)}) %all-reduce.2.cloned.1.call-update) | async-done | bytes 131088 | tf_op jit(solution)/shard_map/psum | solution.py:60
  400.0 1.6 convert_multiply_fusion
  (16 shorter events, 0.1 us)
Async XLA Ops:
  7.2 2.6 copy-start
  7.2 59.3 %all-gather.2.cloned.1.call-start = ((), (), s32[]{:S(2)}) async-start(), calls=%async_computation.1 | async-start | bytes 4718592 | tf_op jit(solution)/shard_map/all_gather | solution.py:37
  10.6 121.7 %reduce-scatter.2.cloned.1.call-start = ((), (), s32[]{:S(2)}) async-start(), calls=%async_computation.2 | async-start | bytes 4718592 | tf_op jit(solution)/shard_map/reduce_scatter | solution.py:45
  66.5 6.8 %copy-start.7 = (bf16[512,4096]{1,0:T(8,128)(2,1)S(1)}, bf16[512,4096]{1,0:T(8,128)(2,1)}, u32[]{:S(2)}) copy-start(bf16[512,4096]{1,0:T(8,128)(2,1)} %param.8) | copy-start | bytes 12582916
  72.4 0.8 copy-start.8
  77.7 0.7 copy-start.6
  77.7 5.1 %copy-start.4 = (f32[128,512]{1,0:T(8,128)S(1)}, f32[128,512]{1,0:T(8,128)}, u32[]{:S(2)}) copy-start(f32[128,512]{1,0:T(8,128)} %param.14) | copy-start | bytes 786436
  77.7 322.3 %all-reduce.2.cloned.1.call-start = ((), (), s32[]{:S(2)}) async-start(), calls=%async_computation.3 | async-start | bytes 262144 | tf_op jit(solution)/shard_map/psum | solution.py:60
  132.3 2.7 copy-start.5
  135.2 1.0 copy-start.3
  135.2 8.1 %copy-start.2 = (f32[4,128,512]{2,1,0:T(8,128)}, f32[4,128,512]{2,1,0:T(8,128)S(1)}, u32[]{:S(2)}) copy-start(f32[4,128,512]{2,1,0:T(8,128)S(1)} %get-tuple-element.12) | copy-start | bytes 3145732
  136.2 7.1 %copy-start.1 = (f32[4,128,512]{2,1,0:T(8,128)}, f32[4,128,512]{2,1,0:T(8,128)S(1)}, u32[]{:S(2)}) copy-start(f32[4,128,512]{2,1,0:T(8,128)S(1)} %get-tuple-element.11) | copy-start | bytes 3145732
Sparse Core Ops, SparseCore 0:
  10.8 55.6 all-gather.1
  77.8 54.4 reduce-scatter.1
  136.4 263.5 all-reduce.1
where the time goes:
time: 409 us; the launch traced here: 408 us
  waiting for transfers between devices  361 us (88%)
  between operations  17.7 us (4%)
  matrix products  17.5 us (4%)
  other arithmetic  6.89 us (2%)
  local copies, waits for them, and re-layouts  4.7 us (1%)
    psum x1, waiting for transfers between devices, body(): lax.psum(pseudo_grad.astype(jnp.bfloat16), 'rep').astype(jnp.float32)  257 us
    all_gather x1, waiting for transfers between devices, body(): gathered = lax.all_gather(weights16, 'fsdp', axis=0, tiled=True)  55.8 us
    reduce_scatter x1, waiting for transfers between devices, body(): lax.psum_scatter(lax.dot_general(activations, cotangent, (((0,), (0,)), (...  48.8 us
  transfers between devices with their start and end apart: 3, of which 3 were waited for; matrix products, arithmetic and copies ran while one was open for 2% of the time, Pallas kernels for 0%

commit v1 on v0

v1 whole, which is shorter than its diff:
```python
import functools

import jax
import jax.numpy as jnp
from jax import lax
from jax.experimental import pallas as pl
from jax.experimental.pallas import tpu as pltpu
from jax.sharding import PartitionSpec as P

DW = 4096
HV = 512
SLAB = 512
TOK = 512
NFRAG = 4
FRAG = SLAB // NFRAG
RA = 288
RB = SLAB - RA
HA = RA // 2
LO = SLAB // 2
ORDER = (6, 5, 7, 2, 4, 1, 3, 0)
FIRST, SECOND, THIRD = (7, 5, 6, 4), (3, 1, 2), (0,)

INNER_RATE = 0.05
INNER_BETA = 0.9
OUTER_RATE = 0.7
OUTER_BETA = 0.9
MIX_SHARE = 0.5
SCALE = DW ** (-0.5)

F32 = jnp.float32
BF16 = jnp.bfloat16
MIB = 1024 * 1024
BIG = 56 * MIB


def move_y(value, step):
    pairs = [(z * 4 + y, z * 4 + (y + step) % 4) for z in range(2) for y in range(4)]
    return lax.ppermute(value, "fsdp", pairs)


def move_z(value):
    return lax.ppermute(value, "fsdp", [(i, (i + 4) % 8) for i in range(8)])


def add16(*terms):
    total = terms[0].astype(F32)
    for term in terms[1:]:
        total = total + term.astype(F32)
    return total


def swap_core(value):
    return lax.ppermute(value, "rep", [(i, i ^ 1) for i in range(32)])


def swap_x(value, flip):
    pairs = []
    for i in range(32):
        x = (i // 2) % 4
        pairs.append((i, i + 2 * ((x ^ flip) - x)))
    return lax.ppermute(value, "rep", pairs)


def swap_z(value, flip):
    pairs = []
    for i in range(32):
        h = i // 8
        pairs.append((i, i + 8 * ((h ^ flip) - h)))
    return lax.ppermute(value, "rep", pairs)


def add_rounded(*terms):
    return add16(*terms).astype(BF16)


def params_of(limit):
    return pltpu.CompilerParams(vmem_limit_bytes=limit)


def turn_kernel(place, x_ref, out_ref):
    out_ref[0] = x_ref[...].T


def turn(place, activations):
    return pl.pallas_call(
        turn_kernel,
        out_shape=jax.ShapeDtypeStruct((8, SLAB, TOK), BF16),
        grid_spec=pltpu.PrefetchScalarGridSpec(
            num_scalar_prefetch=1,
            grid=(8,),
            in_specs=[pl.BlockSpec((TOK, SLAB), lambda d, place: (0, place[d]))],
            out_specs=pl.BlockSpec((1, SLAB, TOK), lambda d, place: (d, 0, 0)),
        ),
        compiler_params=params_of(BIG),
        cost_estimate=pl.CostEstimate(flops=0, bytes_accessed=8 * MIB, transcendentals=0),
    )(place, activations)


def whole(shape):
    return pl.BlockSpec(shape, lambda i, place: (0,) * len(shape))


def forward_kernel(layout, first, last, place, *refs):
    n = len(layout)
    refs = list(refs)
    slabs = [refs.pop(0) for _ in range(n)]
    pieces = [[refs.pop(0) for _ in rows] for rows in layout]
    before = None if first else refs.pop(0)
    target = refs.pop(0) if last else None
    out, weights = refs
    total = None if first else before[...]
    for j in range(n):
        at = 0
        for piece, rows in zip(pieces[j], layout[j]):
            weights[j, at : at + rows, :] = piece[...]
            at += rows
        term = jnp.dot(slabs[j][...], weights[j], preferred_element_type=F32)
        total = term if total is None else total + term
    if last:
        total = (total * SCALE - target[...].astype(F32)).astype(BF16)
    out[...] = total


def forward(place, shards, activations, pieces, before=None, target=None):
    layout = [[p.shape[0] for p in group] for group in pieces]
    n = len(shards)
    slab_specs = [
        pl.BlockSpec((TOK, SLAB), functools.partial(lambda d, i, place: (0, place[d]), d)) for d in shards
    ]
    operands = [p for group in pieces for p in group]
    if before is not None:
        operands.append(before)
    if target is not None:
        operands.append(target)
    out_type = BF16 if target is not None else F32
    return pl.pallas_call(
        functools.partial(forward_kernel, layout, before is None, target is not None),
        out_shape=(
            jax.ShapeDtypeStruct((TOK, HV), out_type),
            jax.ShapeDtypeStruct((n, SLAB, HV), BF16),
        ),
        grid_spec=pltpu.PrefetchScalarGridSpec(
            num_scalar_prefetch=1,
            grid=(1,),
            in_specs=slab_specs + [whole(o.shape) for o in operands],
            out_specs=(whole((TOK, HV)), whole((n, SLAB, HV))),
        ),
        compiler_params=params_of(BIG),
        cost_estimate=pl.CostEstimate(
            flops=2 * n * TOK * SLAB * HV, bytes_accessed=(n + 1) * MIB, transcendentals=0
        ),
    )(place, *([activations] * n), *operands)


def backward_kernel(cuts, turned, cotangent, *outs):
    outs = list(outs)
    for j, rows in enumerate(cuts):
        part = jnp.dot(turned[j], cotangent[...], preferred_element_type=F32).astype(BF16)
        at = 0
        for size in rows:
            outs.pop(0)[...] = part[at : at + size]
            at += size


def backward(turned, cotangent, start, cuts):
    n = len(cuts)
    shapes = [(size, HV) for rows in cuts for size in rows]
    return pl.pallas_call(
        functools.partial(backward_kernel, cuts),
        out_shape=tuple(jax.ShapeDtypeStruct(s, BF16) for s in shapes),
        grid=(1,),
        in_specs=[
            pl.BlockSpec((n, SLAB, TOK), lambda i: (start // n, 0, 0)),
            pl.BlockSpec((TOK, HV), lambda i: (0, 0)),
        ],
        out_specs=tuple(pl.BlockSpec(s, lambda i: (0, 0)) for s in shapes),
        compiler_params=params_of(BIG),
        cost_estimate=pl.CostEstimate(
            flops=2 * n * TOK * SLAB * HV, bytes_accessed=n * MIB, transcendentals=0
        ),
    )(turned, cotangent)


def input_kernel(place, cot, first, second, third, out):
    d = pl.program_id(0)

    def write(weights):
        product = lax.dot_general(
            cot[...], weights[0], (((1,), (1,)), ((), ())), preferred_element_type=F32
        )
        out[...] = (product * SCALE).astype(BF16)

    pl.when(d < 4)(lambda: write(first))
    pl.when((d >= 4) & (d < 7))(lambda: write(second))
    pl.when(d >= 7)(lambda: write(third))


def input_gradient(place, cotangent, first, second, third):
    order = jnp.take(place, jnp.array(FIRST + SECOND + THIRD, jnp.int32))
    return pl.pallas_call(
        input_kernel,
        out_shape=jax.ShapeDtypeStruct((TOK, DW), BF16),
        grid_spec=pltpu.PrefetchScalarGridSpec(
            num_scalar_prefetch=1,
            grid=(8,),
            in_specs=[
                pl.BlockSpec((TOK, HV), lambda d, place: (0, 0)),
                pl.BlockSpec((1, SLAB, HV), lambda d, place: (jnp.minimum(d, 3), 0, 0)),
                pl.BlockSpec((1, SLAB, HV), lambda d, place: (jnp.clip(d - 4, 0, 2), 0, 0)),
                pl.BlockSpec((1, SLAB, HV), lambda d, place: (0, 0, 0)),
            ],
            out_specs=pl.BlockSpec((TOK, SLAB), lambda d, place: (0, place[d])),
        ),
        compiler_params=params_of(BIG),
        cost_estimate=pl.CostEstimate(
            flops=2 * TOK * DW * HV, bytes_accessed=9 * MIB, transcendentals=0
        ),
    )(order, cotangent, first, second, third)


def step_kernel(plan, params, moment, late, *refs):
    *terms, new_params, new_moment = refs
    gradient = add16(*[t[...] for t in terms]) * SCALE
    fresh = INNER_BETA * moment[...] + gradient
    new_moment[...] = fresh
    new_params[...] = params[...] - INNER_RATE * fresh
    rows = pl.ds(pl.multiple_of(plan[0] * FRAG, FRAG), FRAG)
    new_params[rows, :] = MIX_SHARE * new_params[rows, :] + MIX_SHARE * late[...]


def inner_step(plan, params, moment, late, terms):
    operands = [params, moment, late, *terms]
    return pl.pallas_call(
        step_kernel,
        out_shape=(jax.ShapeDtypeStruct((SLAB, HV), F32),) * 2,
        grid_spec=pltpu.PrefetchScalarGridSpec(
            num_scalar_prefetch=1,
            grid=(1,),
            in_specs=[whole(o.shape) for o in operands],
            out_specs=(whole((SLAB, HV)),) * 2,
        ),
        compiler_params=params_of(BIG),
        cost_estimate=pl.CostEstimate(flops=0, bytes_accessed=6 * MIB, transcendentals=0),
    )(plan, *operands)


def outer_kernel(plan, outer, moment, pending, new_outer, new_moment, late):
    rows = pl.ds(pl.multiple_of(plan[0] * FRAG, FRAG), FRAG)
    arrived = pending[...]
    new_outer[...] = outer[...]
    new_moment[...] = moment[...]
    moment_late = OUTER_BETA * moment[rows, :] + arrived
    outer_late = outer[rows, :] - OUTER_RATE * (arrived + OUTER_BETA * moment_late)
    new_moment[rows, :] = moment_late
    new_outer[rows, :] = outer_late
    late[...] = outer_late


def outer_step(plan, outer, moment, pending):
    operands = [outer, moment, pending]
    return pl.pallas_call(
        outer_kernel,
        out_shape=(
            jax.ShapeDtypeStruct((SLAB, HV), F32),
            jax.ShapeDtypeStruct((SLAB, HV), F32),
            jax.ShapeDtypeStruct((FRAG, HV), F32),
        ),
        grid_spec=pltpu.PrefetchScalarGridSpec(
            num_scalar_prefetch=1,
            grid=(1,),
            in_specs=[whole(o.shape) for o in operands],
            out_specs=(whole((SLAB, HV)), whole((SLAB, HV)), whole((FRAG, HV))),
        ),
        compiler_params=params_of(BIG),
        cost_estimate=pl.CostEstimate(flops=0, bytes_accessed=5 * MIB, transcendentals=0),
    )(plan, *operands)


def local_fragment(matrix, frag_index):
    return lax.dynamic_slice_in_dim(matrix, frag_index * FRAG, FRAG, 0)


def after(value, *others):
    return lax.optimization_barrier((value, *others))[0]


def body(activations, target, params, momentum, outer_params, outer_momentum, pending, plan):
    weights, moment = params[0], momentum[0]
    me, rep = lax.axis_index("fsdp"), lax.axis_index("rep")
    core = rep % 2
    relative = jnp.array(ORDER, jnp.int32)
    place = ((me // 4 + relative // 4) % 2) * 4 + (me % 4 + relative % 4) % 4

    w = weights.astype(BF16)
    w_back, w_next, w_z = move_y(w, 1), move_y(w, -1), move_z(w)

    turned = turn(place, after(activations, w))
    leaving = local_fragment(outer_params, plan[2]) - local_fragment(after(weights, w), plan[2])
    leaving = leaving.astype(BF16)
    half = FRAG // 2
    mine = lax.dynamic_slice_in_dim(leaving, core * half, half, 0)
    theirs = lax.dynamic_slice_in_dim(leaving, (1 - core) * half, half, 0)
    share = add_rounded(mine, swap_core(theirs))
    new_outer, new_outer_momentum, outer_late = outer_step(
        plan, after(outer_params, turned), outer_momentum, pending
    )

    a_z = w_z[:RA]
    az_back, az_next = move_y(a_z, 1), move_y(a_z, -1)
    far_lo, far_hi = move_y(w_back[:LO], 1), move_y(w_next[LO:], -1)
    bz_next, bz_back = move_z(w_next[RA:]), move_z(w_back[RA:])
    values, w_first = forward(place, FIRST, activations, [[w], [w_next], [w_back], [w_z]])
    share = add_rounded(share, swap_x(after(share, w_z), 1))
    share = add_rounded(share, swap_x(share, 3))

    az_lo, az_hi = move_y(az_back[:HA], 1), move_y(az_next[HA:], -1)
    bz_far = move_z(far_hi[RA - LO :])
    values, w_second = forward(
        place,
        SECOND,
        activations,
        [[far_lo, far_hi], [az_next, bz_next], [az_back, bz_back]],
        before=values,
    )
    cotangent, w_third = forward(
        place, THIRD, activations, [[az_lo, az_hi, bz_far]], before=values, target=target
    )

    z12_lo, z12_hi, z12_b, z11_a, z11_b, z13_a, z13_b, z02_lo, z02_hi = backward(
        turned, cotangent, 0, [[HA, HA, RB], [RA, RB], [RA, RB], [LO, SLAB - LO]]
    )
    z10, z01, z03, z00 = backward(turned, cotangent, 4, [[SLAB]] * 4)
    in11_lo, in13_hi = move_y(z12_lo, 1), move_y(z12_hi, -1)
    in02_b, in01_b, in03_b = move_z(z12_b), move_z(z11_b), move_z(z13_b)
    in01_lo = move_y(z02_lo, 1)

    grad_input = input_gradient(place, cotangent, w_first, w_second, w_third)

    to_next = jnp.concatenate([add_rounded(z11_a[:HA], in11_lo), z11_a[HA:]], 0)
    to_back = jnp.concatenate([z13_a[:HA], add_rounded(z13_a[HA:], in13_hi)], 0)
    in10_back, in10_next = move_y(to_next, 1), move_y(to_back, -1)
    in03_hi = move_y(jnp.concatenate([z02_hi[: RA - LO], add_rounded(z02_hi[RA - LO :], in02_b)], 0), -1)

    share = add_rounded(share, swap_z(after(share, in01_b), 1))
    share = add_rounded(share, swap_z(share, 3))

    z01, z03, z10 = after((z01, z03, z10), grad_input)
    to_next = jnp.concatenate(
        [add_rounded(z01[:LO], in01_lo), z01[LO:RA], add_rounded(z01[RA:], in01_b)], 0
    )
    to_back = jnp.concatenate(
        [
            z03[:LO],
            add_rounded(z03[LO:RA], in03_hi[: RA - LO]),
            add_rounded(z03[RA:], in03_hi[RA - LO :], in03_b),
        ],
        0,
    )
    in00_back, in00_next = move_y(to_next, 1), move_y(to_back, -1)
    across = jnp.concatenate([add_rounded(z10[:RA], in10_back, in10_next), z10[RA:]], 0)
    in00_z = move_z(across)

    other = swap_core(share)
    low, high = jnp.where(core == 0, share, other), jnp.where(core == 0, other, share)
    new_pending = jnp.concatenate([low, high], 0).astype(F32) / lax.axis_size("rep")

    new_params, new_moment = inner_step(
        plan, weights, moment, outer_late, [z00, in00_back, in00_next, in00_z]
    )
    return (
        new_params[None],
        new_moment[None],
        grad_input,
        new_outer,
        new_outer_momentum,
        new_pending,
    )


def solution(mesh):
    placed = (
        P(("rep", "fsdp"), None),
        P(("rep", "fsdp"), None),
        P("rep", "fsdp", None),
        P("rep", "fsdp", None),
        P("fsdp", None),
        P("fsdp", None),
        P("fsdp", None),
        P(),
    )
    return jax.shard_map(
        body,
        mesh=mesh,
        in_specs=placed,
        out_specs=(
            P("rep", "fsdp", None),
            P("rep", "fsdp", None),
            P(("rep", "fsdp"), None),
            P("fsdp", None),
            P("fsdp", None),
            P("fsdp", None),
        ),
        check_vma=False,
    )
```

time: 409 us -> 124 us (0.30)
  waiting for transfers between devices: 361 us -> 18.9 us
  Pallas kernels: 0 us -> 46.9 us
  starting transfers between devices: 0.12 us -> 41.7 us
  matrix products: 17.5 us -> 0 us
  between operations: 17.7 us -> 1.85 us
    psum x1 -> x0, waiting for transfers between devices: 257 us -> none  [body(): lax.psum(pseudo_grad.astype(jnp.bfloat16), 'rep').astype(jnp.float32)]
    all_gather x1 -> x0, waiting for transfers between devices: 55.8 us -> none  [body(): gathered = lax.all_gather(weights16, 'fsdp', axis=0, tiled=True)]
    reduce_scatter x1 -> x0, waiting for transfers between devices: 48.8 us -> none  [body(): lax.psum_scatter(lax.dot_general(activations, cotangent, (((0,), (0,)), (...]
    pallas_call x0 -> x9, Pallas kernels: none -> 46.9 us  [the longest x3 14 us: forward(): pl.pallas_call(functools.partial(forward_kernel, layout, before is None,...]
    ppermute x0 -> x30, starting transfers between devices: none -> 41.7 us  [the longest x16 19.4 us: move_y(): return lax.ppermute(value, 'fsdp', pairs)]
    ppermute x0 -> x30, waiting for transfers between devices: none -> 18.9 us  [the longest x16 8.95 us: move_y(): return lax.ppermute(value, 'fsdp', pairs)]
    dot_general x3 -> x0, matrix products: 17.5 us -> none  [the longest x1 7.11 us: body(): lax.dot_general(cotangent, gathered, (((1,), (1,)), ((), ())), preferred_...]
    slice x1 -> x15, local copies, waits for them, and re-layouts: 0.58 us -> 5.09 us  [the longest x1 1.24 us: body(): plan[2]]
  transfers between devices with their start and end apart: 3 -> 30, of which waited for: 3 -> 8; matrix products, arithmetic and copies ran while one was open for 2% -> 8% of each run, Pallas kernels for 0% -> 28%
where the time goes in v1:
time: 124 us; the launch traced here: 123 us
  Pallas kernels  46.9 us (38%)
  starting transfers between devices  41.7 us (34%)
  waiting for transfers between devices  18.9 us (15%)
  local copies, waits for them, and re-layouts  8.67 us (7%)
  other arithmetic  5.19 us (4%)
  between operations  1.85 us (1%)
    ppermute x16, starting transfers between devices, move_y(): return lax.ppermute(value, 'fsdp', pairs)  19.4 us
    pallas_call x3, Pallas kernels, forward(): pl.pallas_call(functools.partial(forward_kernel, layout, before is None,...  14 us
    ppermute x8, starting transfers between devices, move_z(): return lax.ppermute(value, 'fsdp', [(i, (i + 4) % 8) for i in range(8)])  9.41 us
    ppermute x2, starting transfers between devices, swap_z(): return lax.ppermute(value, 'rep', pairs)  9.05 us
    ppermute x16, waiting for transfers between devices, move_y(): return lax.ppermute(value, 'fsdp', pairs)  8.95 us
    pallas_call x1, Pallas kernels, input_gradient(): pl.pallas_call(input_kernel, out_shape=jax.ShapeDtypeStruct((TOK, DW), BF...  8.8 us
    pallas_call x1, Pallas kernels, turn(): pl.pallas_call(turn_kernel, out_shape=jax.ShapeDtypeStruct((8, SLAB, TOK)...  7.87 us
    pallas_call x2, Pallas kernels, backward(): pl.pallas_call(functools.partial(backward_kernel, cuts), out_shape=tuple(...  7.52 us
  transfers between devices with their start and end apart: 30, of which 8 were waited for; matrix products, arithmetic and copies ran while one was open for 8% of the time, Pallas kernels for 28%

profile of v1, /device:TPU:24, one launch (start us, length us, event | category | flops | bytes accessed | tf_op | source)
XLA Modules:
  0.0 123.3 jit_solution(12850957733032402859)
XLA Ops:
  1.9 2.0 %collective-permute-start.8 = (bf16[512,512]{1,0:T(8,128)(2,1)S(1)}, bf16[512,512]{1,0:T(8,128)(2,1)S(1)}, u32[]{:S(2)}, u32[]{:S(2)}) collective-permute-start(bf16[512,512]{1,0:T(8,128)(2,1)S(1)} %bitcast_convert_fusion.refs_4_), channel_id=1, source_target_pairs={{0,1},{1,2},{2,3},{3,0},{4,5},{5,6},{6,7},{7,4},{8,9},{9,10},{10,1... | collective-permute-start | bytes 1572872 | tf_op jit(solution)/shard_map/ppermute | solution.py:38
  10.3 6.7 %collective-permute-done.5.refs_5_ = bf16[512,512]{1,0:T(8,128)(2,1)S(1)} collective-permute-done((bf16[512,512]{1,0:T(8,128)(2,1)S(1)}, bf16[512,512]{1,0:T(8,128)(2,1)S(1)}, u32[]{:S(2)}, u32[]{:S(2)}) %collective-permute-start.5) | collective-permute-done | bytes 524320 | tf_op jit(solution)/shard_map/ppermute | solution.py:38
  20.9 7.9 %shard_map.145.turned = bf16[8,512,512]{2,1,0:T(8,128)(2,1)} custom-call(s32[8]{0:T(128)} %copy-done, bf16[512,4096]{1,0:T(8,128)(2,1)} %refs_0_.5), custom_call_target="tpu_custom_call" | custom-call | bytes 8388608 | tf_op jit(solution)/shard_map/pallas_call | solution.py:85
  29.6 2.5 %collective-permute-start.1 = (bf16[288,512]{1,0:T(8,128)(2,1)S(1)}, bf16[288,512]{1,0:T(8,128)(2,1)S(1)}, u32[]{:S(2)}, u32[]{:S(2)}) collective-permute-start(bf16[288,512]{1,0:T(8,128)(2,1)S(1)} %slice.103), channel_id=1, source_target_pairs={{0,1},{1,2},{2,3},{3,0},{4,5},{5,6},{6,7},{7,4},{8,9},{9,10},{10,1... | collective-permute-start | bytes 884744 | tf_op jit(solution)/shard_map/ppermute | solution.py:38
  32.1 2.0 %collective-permute-start.11 = (bf16[224,512]{1,0:T(8,128)(2,1)S(1)}, bf16[224,512]{1,0:T(8,128)(2,1)S(1)}, u32[]{:S(2)}, u32[]{:S(2)}) collective-permute-start(bf16[224,512]{1,0:T(8,128)(2,1)S(1)} %slice.110), channel_id=1, source_target_pairs={{0,4},{1,5},{2,6},{3,7},{4,0},{5,1},{6,2},{7,3},{8,12},{9,13},{10,... | collective-permute-start | bytes 688136 | tf_op jit(solution)/shard_map/ppermute | solution.py:42
  35.8 2.2 %collective-permute-start.26 = (bf16[64,512]{1,0:T(8,128)(2,1)S(1)}, bf16[64,512]{1,0:T(8,128)(2,1)S(1)}, u32[]{:S(2)}, u32[]{:S(2)}) collective-permute-start(bf16[64,512]{1,0:T(8,128)(2,1)S(1)} %add_convert_fusion.10), channel_id=1, source_target_pairs={{0,48},{8,56},{16,32},{24,40},{32,16},{40,24},{48,0},{56,8},{64,11... | collective-permute-start | bytes 196616 | tf_op jit(solution)/shard_map/ppermute | solution.py:61
  38.0 5.4 %shard_map.147 = (f32[512,512]{1,0:T(8,128)}, bf16[4,512,512]{2,1,0:T(8,128)(2,1)}) custom-call(s32[8]{0:T(128)} %copy-done, bf16[512,4096]{1,0:T(8,128)(2,1)} %refs_0_.5, bf16[512,4096]{1,0:T(8,128)(2,1)} %refs_0_.5, bf16[512,4096]{1,0:T(8,128)(2,1)} %refs_0_.5, bf16[512,4096]{1,0:T(8,128)(2,1)} %refs_0_.5, bf16[512,512]{1,0:T(8,128)(2,1)} %copy-done.1, ...), custom_call_target="tpu_custom_call" | custom-call | flops 1073741824 | bytes 5242880 | tf_op jit(solution)/shard_map/pallas_call | solution.py:136
  44.7 2.0 %collective-permute-start.7 = (bf16[224,512]{1,0:T(8,128)(2,1)S(1)}, bf16[224,512]{1,0:T(8,128)(2,1)S(1)}, u32[]{:S(2)}, u32[]{:S(2)}) collective-permute-start(bf16[224,512]{1,0:T(8,128)(2,1)S(1)} %slice.107), channel_id=1, source_target_pairs={{0,4},{1,5},{2,6},{3,7},{4,0},{5,1},{6,2},{7,3},{8,12},{9,13},{10,... | collective-permute-start | bytes 688136 | tf_op jit(solution)/shard_map/ppermute | solution.py:42
  47.2 2.8 %collective-permute-start.2 = (bf16[144,512]{1,0:T(8,128)(2,1)S(1)}, bf16[144,512]{1,0:T(8,128)(2,1)S(1)}, u32[]{:S(2)}, u32[]{:S(2)}) collective-permute-start(bf16[144,512]{1,0:T(8,128)(2,1)S(1)} %slice.104), channel_id=1, source_target_pairs={{0,1},{1,2},{2,3},{3,0},{4,5},{5,6},{6,7},{7,4},{8,9},{9,10},{10,1... | collective-permute-start | bytes 442376 | tf_op jit(solution)/shard_map/ppermute | solution.py:38
  52.1 5.0 %shard_map.148 = (f32[512,512]{1,0:T(8,128)}, bf16[3,512,512]{2,1,0:T(8,128)(2,1)}) custom-call(s32[8]{0:T(128)} %copy-done, bf16[512,4096]{1,0:T(8,128)(2,1)} %refs_0_.5, bf16[512,4096]{1,0:T(8,128)(2,1)} %refs_0_.5, bf16[512,4096]{1,0:T(8,128)(2,1)} %refs_0_.5, bf16[256,512]{1,0:T(8,128)(2,1)} %copy-done.16, bf16[256,512]{1,0:T(8,128)(2,1)} %copy-done.5, ...), custom_call_target="tpu_custom_call" | custom-call | flops 805306368 | bytes 4194304 | tf_op jit(solution)/shard_map/pallas_call | solution.py:136
  57.9 3.7 %shard_map.149 = (bf16[512,512]{1,0:T(8,128)(2,1)}, bf16[1,512,512]{2,1,0:T(8,128)(2,1)}) custom-call(s32[8]{0:T(128)} %copy-done, bf16[512,4096]{1,0:T(8,128)(2,1)} %refs_0_.5, bf16[144,512]{1,0:T(8,128)(2,1)} %copy-done.22, bf16[144,512]{1,0:T(8,128)(2,1)} %copy-done.21, bf16[224,512]{1,0:T(8,128)(2,1)} %copy-done.20, ...), custom_call_target="tpu_custom_call" | custom-call | flops 268435456 | bytes 2097152 | tf_op jit(solution)/shard_map/pallas_call | solution.py:136
  61.6 3.6 %shard_map.152 = (bf16[144,512]{1,0:T(8,128)(2,1)}, bf16[144,512]{1,0:T(8,128)(2,1)}, bf16[224,512]{1,0:T(8,128)(2,1)}, bf16[288,512]{1,0:T(8,128)(2,1)}, bf16[2...) custom-call(bf16[8,512,512]{2,1,0:T(8,128)(2,1)} %shard_map.145.turn, ...), custom_call_target="tpu_custom_call" | custom-call | flops 1073741824 | bytes 4194304 | tf_op jit(solution)/shard_map/pallas_call | solution.py:168
  65.6 8.8 %shard_map.151 = bf16[512,4096]{1,0:T(8,128)(2,1)} custom-call(s32[8]{0:T(128)} %gather_fusion, bf16[512,512]{1,0:T(8,128)(2,1)} %get-tuple-element.43.cotangent.cot, bf16[4,512,512]{2,1,0:T(8,128)(2,1)} %get-tuple-element.48.first, bf16[3,512,512]{2,1,0:T(8,128)(2,1)} %get-tuple-element.49.second, bf16[1,512,512]{2,1,0:T(8,128)(2,1)} %get-tuple-element.50.third), custom_call_target="tpu_custom_call" | custom-call | flops 2147483648 | bytes 9437184 | tf_op jit(solution)/shard_map/pallas_call | solution.py:200
  74.5 3.9 %shard_map.150 = (bf16[512,512]{1,0:T(8,128)(2,1)}, bf16[512,512]{1,0:T(8,128)(2,1)}, bf16[512,512]{1,0:T(8,128)(2,1)}, bf16[512,512]{1,0:T(8,128)(2,1)}) custom-call(bf16[8,512,512]{2,1,0:T(8,128)(2,1)} %shard_map.145.turned, bf16[512,512]{1,0:T(8,128)(2,1)} %get-tuple-element.43.cotangent.cot), custom_call_target="tpu_custom_call" | custom-call | flops 1073741824 | bytes 4194304 | tf_op jit(solution)/shard_map/pallas_call | solution.py:168
  79.3 2.9 %collective-permute-start.19 = (bf16[144,512]{1,0:T(8,128)(2,1)S(1)}, bf16[144,512]{1,0:T(8,128)(2,1)S(1)}, u32[]{:S(2)}, u32[]{:S(2)}) collective-permute-start(bf16[144,512]{1,0:T(8,128)(2,1)S(1)} %copy-done.27), channel_id=1, source_target_pairs={{0,1},{1,2},{2,3},{3,0},{4,5},{5,6},{6,7},{7,4},{8,9},{9,10},{10,1... | collective-permute-start | bytes 442376 | tf_op jit(solution)/shard_map/ppermute | solution.py:38
  86.8 2.1 %collective-permute-start.22 = (bf16[288,512]{1,0:T(8,128)(2,1)S(1)}, bf16[288,512]{1,0:T(8,128)(2,1)S(1)}, u32[]{:S(2)}, u32[]{:S(2)}) collective-permute-start(bf16[288,512]{1,0:T(8,128)(2,1)S(1)} %pad_maximum_fusion.4), channel_id=1, source_target_pairs={{0,3},{1,0},{2,1},{3,2},{4,7},{5,4},{6,5},{7,6},{8,11},{9,8},{10,9... | collective-permute-start | bytes 884744 | tf_op jit(solution)/shard_map/ppermute | solution.py:38
  91.0 2.2 %collective-permute-done.15 = bf16[224,512]{1,0:T(8,128)(2,1)S(1)} collective-permute-done((bf16[224,512]{1,0:T(8,128)(2,1)S(1)}, bf16[224,512]{1,0:T(8,128)(2,1)S(1)}, u32[]{:S(2)}, u32[]{:S(2)}) %collective-permute-start.15) | collective-permute-done | bytes 229408 | tf_op jit(solution)/shard_map/ppermute | solution.py:42
  93.2 3.3 %collective-permute-start.27 = (bf16[64,512]{1,0:T(8,128)(2,1)S(1)}, bf16[64,512]{1,0:T(8,128)(2,1)S(1)}, u32[]{:S(2)}, u32[]{:S(2)}) collective-permute-start(bf16[64,512]{1,0:T(8,128)(2,1)S(1)} %add_convert_fusion.9), channel_id=1, source_target_pairs={{0,64},{8,72},{16,80},{24,88},{32,96},{40,104},{48,112},{56,120},{... | collective-permute-start | bytes 196616 | tf_op jit(solution)/shard_map/ppermute | solution.py:69
  96.8 2.0 %collective-permute-done.27 = bf16[64,512]{1,0:T(8,128)(2,1)S(1)} collective-permute-done((bf16[64,512]{1,0:T(8,128)(2,1)S(1)}, bf16[64,512]{1,0:T(8,128)(2,1)S(1)}, u32[]{:S(2)}, u32[]{:S(2)}) %collective-permute-start.27) | collective-permute-done | bytes 65568 | tf_op jit(solution)/shard_map/ppermute | solution.py:69
  100.2 5.8 %collective-permute-start.28 = (bf16[64,512]{1,0:T(8,128)(2,1)S(1)}, bf16[64,512]{1,0:T(8,128)(2,1)S(1)}, u32[]{:S(2)}, u32[]{:S(2)}) collective-permute-start(bf16[64,512]{1,0:T(8,128)(2,1)S(1)} %add_convert_fusion.8), channel_id=1, source_target_pairs={{0,192},{8,200},{16,208},{24,216},{32,224},{40,232},{48,240},{56,2... | collective-permute-start | bytes 196616 | tf_op jit(solution)/shard_map/ppermute | solution.py:69
  108.6 3.9 %shard_map.146 = (f32[512,512]{1,0:T(8,128)}, f32[512,512]{1,0:T(8,128)}, f32[128,512]{1,0:T(8,128)}) custom-call(s32[4]{0:T(128)} %plan.3, f32[512,512]{1,0:T(8,128)} %outer, f32[512,512]{1,0:T(8,128)} %moment.1, f32[128,512]{1,0:T(8,128)} %pending.1), custom_call_target="tpu_custom_call" | custom-call | bytes 5242880 | tf_op jit(solution)/shard_map/pallas_call | solution.py:261
  113.3 2.1 %collective-permute-done.23.refs_3_ = bf16[512,512]{1,0:T(8,128)(2,1)S(1)} collective-permute-done((bf16[512,512]{1,0:T(8,128)(2,1)S(1)}, bf16[512,512]{1,0:T(8,128)(2,1)S(1)}, u32[]{:S(2)}, u32[]{:S(2)}) %collective-permute-start.23) | collective-permute-done | bytes 524320 | tf_op jit(solution)/shard_map/ppermute | solution.py:42
  115.4 2.2 %collective-permute-done.18.refs_2_ = bf16[512,512]{1,0:T(8,128)(2,1)S(1)} collective-permute-done((bf16[512,512]{1,0:T(8,128)(2,1)S(1)}, bf16[512,512]{1,0:T(8,128)(2,1)S(1)}, u32[]{:S(2)}, u32[]{:S(2)}) %collective-permute-start.18) | collective-permute-done | bytes 524320 | tf_op jit(solution)/shard_map/ppermute | solution.py:38
  118.4 4.8 %shard_map.153 = (f32[512,512]{1,0:T(8,128)}, f32[512,512]{1,0:T(8,128)}) custom-call(s32[4]{0:T(128)} %plan.3, f32[512,512]{1,0:T(8,128)} %bitcast.7, f32[512,512]{1,0:T(8,128)} %bitcast.8, f32[128,512]{1,0:T(8,128)} %get-tuple-element.40.late, bf16[512,512]{1,0:T(8,128)(2,1)} %get-tuple-element.44.refs_0_, bf16[512,512]{1,0:T(8,128)(2,1)} %copy-done.8, ...), custom_call_target="tpu_custom_call" | custom-call | bytes 6291456 | tf_op jit(solution)/shard_map/pallas_call | solution.py:233
  (143 shorter events, 31.7 us)
Async XLA Ops:
  1.9 30.2 %collective-permute-start.8 = (bf16[512,512]{1,0:T(8,128)(2,1)S(1)}, bf16[512,512]{1,0:T(8,128)(2,1)S(1)}, u32[]{:S(2)}, u32[]{:S(2)}) collective-permute-start(bf16[512,512]{1,0:T(8,128)(2,1)S(1)} %bitcast_convert_fusion.refs_4_), channel_id=1, source_target_pairs={{0,1},{1,2},{2,3},{3,0},{4,5},{5,6},{6,7},{7,4},{8,9},{9,10},{10,1... | collective-permute-start | bytes 1572872 | tf_op jit(solution)/shard_map/ppermute | solution.py:38
  4.0 13.0 %collective-permute-start.5 = (bf16[512,512]{1,0:T(8,128)(2,1)S(1)}, bf16[512,512]{1,0:T(8,128)(2,1)S(1)}, u32[]{:S(2)}, u32[]{:S(2)}) collective-permute-start(bf16[512,512]{1,0:T(8,128)(2,1)S(1)} %bitcast_convert_fusion.refs_4_), channel_id=1, source_target_pairs={{0,3},{1,0},{2,1},{3,2},{4,7},{5,4},{6,5},{7,6},{8,11},{9,8},{10,9... | collective-permute-start | bytes 1572872 | tf_op jit(solution)/shard_map/ppermute | solution.py:38
  4.0 13.5 %collective-permute-start = (bf16[512,512]{1,0:T(8,128)(2,1)S(1)}, bf16[512,512]{1,0:T(8,128)(2,1)S(1)}, u32[]{:S(2)}, u32[]{:S(2)}) collective-permute-start(bf16[512,512]{1,0:T(8,128)(2,1)S(1)} %bitcast_convert_fusion.refs_4_), channel_id=1, source_target_pairs={{0,4},{1,5},{2,6},{3,7},{4,0},{5,1},{6,2},{7,3},{8,12},{9,13},{10,... | collective-permute-start | bytes 1572872 | tf_op jit(solution)/shard_map/ppermute | solution.py:42
  17.0 18.8 %collective-permute-start.6 = (bf16[256,512]{1,0:T(8,128)(2,1)S(1)}, bf16[256,512]{1,0:T(8,128)(2,1)S(1)}, u32[]{:S(2)}, u32[]{:S(2)}) collective-permute-start(bf16[256,512]{1,0:T(8,128)(2,1)S(1)} %slice.106), channel_id=1, source_target_pairs={{0,3},{1,0},{2,1},{3,2},{4,7},{5,4},{6,5},{7,6},{8,11},{9,8},{10,9... | collective-permute-start | bytes 786440 | tf_op jit(solution)/shard_map/ppermute | solution.py:38
  17.5 16.6 %collective-permute-start.25 = (bf16[64,512]{1,0:T(8,128)(2,1)S(1)}, bf16[64,512]{1,0:T(8,128)(2,1)S(1)}, u32[]{:S(2)}, u32[]{:S(2)}) collective-permute-start(bf16[64,512]{1,0:T(8,128)(2,1)S(1)} %add_convert_fusion.11), channel_id=1, source_target_pairs={{0,16},{8,24},{16,0},{24,8},{32,48},{40,56},{48,32},{56,40},{64,80... | collective-permute-start | bytes 196616 | tf_op jit(solution)/shard_map/ppermute | solution.py:61
  28.8 15.6 %collective-permute-start.3 = (bf16[288,512]{1,0:T(8,128)(2,1)S(1)}, bf16[288,512]{1,0:T(8,128)(2,1)S(1)}, u32[]{:S(2)}, u32[]{:S(2)}) collective-permute-start(bf16[288,512]{1,0:T(8,128)(2,1)S(1)} %slice.103), channel_id=1, source_target_pairs={{0,3},{1,0},{2,1},{3,2},{4,7},{5,4},{6,5},{7,6},{8,11},{9,8},{10,9... | collective-permute-start | bytes 884744 | tf_op jit(solution)/shard_map/ppermute | solution.py:38
  29.6 15.1 %collective-permute-start.1 = (bf16[288,512]{1,0:T(8,128)(2,1)S(1)}, bf16[288,512]{1,0:T(8,128)(2,1)S(1)}, u32[]{:S(2)}, u32[]{:S(2)}) collective-permute-start(bf16[288,512]{1,0:T(8,128)(2,1)S(1)} %slice.103), channel_id=1, source_target_pairs={{0,1},{1,2},{2,3},{3,0},{4,5},{5,6},{6,7},{7,4},{8,9},{9,10},{10,1... | collective-permute-start | bytes 884744 | tf_op jit(solution)/shard_map/ppermute | solution.py:38
  32.1 15.1 %collective-permute-start.11 = (bf16[224,512]{1,0:T(8,128)(2,1)S(1)}, bf16[224,512]{1,0:T(8,128)(2,1)S(1)}, u32[]{:S(2)}, u32[]{:S(2)}) collective-permute-start(bf16[224,512]{1,0:T(8,128)(2,1)S(1)} %slice.110), channel_id=1, source_target_pairs={{0,4},{1,5},{2,6},{3,7},{4,0},{5,1},{6,2},{7,3},{8,12},{9,13},{10,... | collective-permute-start | bytes 688136 | tf_op jit(solution)/shard_map/ppermute | solution.py:42
  34.1 17.2 %collective-permute-start.9 = (bf16[256,512]{1,0:T(8,128)(2,1)S(1)}, bf16[256,512]{1,0:T(8,128)(2,1)S(1)}, u32[]{:S(2)}, u32[]{:S(2)}) collective-permute-start(bf16[256,512]{1,0:T(8,128)(2,1)S(1)} %slice.108), channel_id=1, source_target_pairs={{0,1},{1,2},{2,3},{3,0},{4,5},{5,6},{6,7},{7,4},{8,9},{9,10},{10,1... | collective-permute-start | bytes 786440 | tf_op jit(solution)/shard_map/ppermute | solution.py:38
  35.8 10.8 %collective-permute-start.26 = (bf16[64,512]{1,0:T(8,128)(2,1)S(1)}, bf16[64,512]{1,0:T(8,128)(2,1)S(1)}, u32[]{:S(2)}, u32[]{:S(2)}) collective-permute-start(bf16[64,512]{1,0:T(8,128)(2,1)S(1)} %add_convert_fusion.10), channel_id=1, source_target_pairs={{0,48},{8,56},{16,32},{24,40},{32,16},{40,24},{48,0},{56,8},{64,11... | collective-permute-start | bytes 196616 | tf_op jit(solution)/shard_map/ppermute | solution.py:61
  44.7 12.5 %collective-permute-start.7 = (bf16[224,512]{1,0:T(8,128)(2,1)S(1)}, bf16[224,512]{1,0:T(8,128)(2,1)S(1)}, u32[]{:S(2)}, u32[]{:S(2)}) collective-permute-start(bf16[224,512]{1,0:T(8,128)(2,1)S(1)} %slice.107), channel_id=1, source_target_pairs={{0,4},{1,5},{2,6},{3,7},{4,0},{5,1},{6,2},{7,3},{8,12},{9,13},{10,... | collective-permute-start | bytes 688136 | tf_op jit(solution)/shard_map/ppermute | solution.py:42
  46.7 10.4 %collective-permute-start.4 = (bf16[144,512]{1,0:T(8,128)(2,1)S(1)}, bf16[144,512]{1,0:T(8,128)(2,1)S(1)}, u32[]{:S(2)}, u32[]{:S(2)}) collective-permute-start(bf16[144,512]{1,0:T(8,128)(2,1)S(1)} %slice.105), channel_id=1, source_target_pairs={{0,3},{1,0},{2,1},{3,2},{4,7},{5,4},{6,5},{7,6},{8,11},{9,8},{10,9... | collective-permute-start | bytes 442376 | tf_op jit(solution)/shard_map/ppermute | solution.py:38
  47.2 9.9 %collective-permute-start.2 = (bf16[144,512]{1,0:T(8,128)(2,1)S(1)}, bf16[144,512]{1,0:T(8,128)(2,1)S(1)}, u32[]{:S(2)}, u32[]{:S(2)}) collective-permute-start(bf16[144,512]{1,0:T(8,128)(2,1)S(1)} %slice.104), channel_id=1, source_target_pairs={{0,1},{1,2},{2,3},{3,0},{4,5},{5,6},{6,7},{7,4},{8,9},{9,10},{10,1... | collective-permute-start | bytes 442376 | tf_op jit(solution)/shard_map/ppermute | solution.py:38
  65.2 21.4 %collective-permute-start.21 = (bf16[144,512]{1,0:T(8,128)(2,1)}, bf16[144,512]{1,0:T(8,128)(2,1)S(1)}, u32[]{:S(2)}, u32[]{:S(2)}) collective-permute-start(bf16[144,512]{1,0:T(8,128)(2,1)} %get-tuple-element.62), channel_id=1, source_target_pairs={{0,3},{1,0},{2,1},{3,2},{4,7},{5,4},{6,5},{7,6},{8,11},{9,8},{10,9... | collective-permute-start | bytes 442376 | tf_op jit(solution)/shard_map/ppermute | solution.py:38
  83.6 9.6 %collective-permute-start.15 = (bf16[224,512]{1,0:T(8,128)(2,1)S(1)}, bf16[224,512]{1,0:T(8,128)(2,1)S(1)}, u32[]{:S(2)}, u32[]{:S(2)}) collective-permute-start(bf16[224,512]{1,0:T(8,128)(2,1)S(1)} %copy-done.25), channel_id=1, source_target_pairs={{0,4},{1,5},{2,6},{3,7},{4,0},{5,1},{6,2},{7,3},{8,12},{9,13},{10,... | collective-permute-start | bytes 688136 | tf_op jit(solution)/shard_map/ppermute | solution.py:42
  85.3 21.7 %collective-permute-start.17 = (bf16[224,512]{1,0:T(8,128)(2,1)S(1)}, bf16[224,512]{1,0:T(8,128)(2,1)S(1)}, u32[]{:S(2)}, u32[]{:S(2)}) collective-permute-start(bf16[224,512]{1,0:T(8,128)(2,1)S(1)} %copy-done.24), channel_id=1, source_target_pairs={{0,4},{1,5},{2,6},{3,7},{4,0},{5,1},{6,2},{7,3},{8,12},{9,13},{10,... | collective-permute-start | bytes 688136 | tf_op jit(solution)/shard_map/ppermute | solution.py:42
  86.6 10.0 %collective-permute-start.12 = (bf16[256,512]{1,0:T(8,128)(2,1)S(1)}, bf16[256,512]{1,0:T(8,128)(2,1)S(1)}, u32[]{:S(2)}, u32[]{:S(2)}) collective-permute-start(bf16[256,512]{1,0:T(8,128)(2,1)S(1)} %copy-done.23), channel_id=1, source_target_pairs={{0,1},{1,2},{2,3},{3,0},{4,5},{5,6},{6,7},{7,4},{8,9},{9,10},{10,1... | collective-permute-start | bytes 786440 | tf_op jit(solution)/shard_map/ppermute | solution.py:38
  86.8 13.4 %collective-permute-start.22 = (bf16[288,512]{1,0:T(8,128)(2,1)S(1)}, bf16[288,512]{1,0:T(8,128)(2,1)S(1)}, u32[]{:S(2)}, u32[]{:S(2)}) collective-permute-start(bf16[288,512]{1,0:T(8,128)(2,1)S(1)} %pad_maximum_fusion.4), channel_id=1, source_target_pairs={{0,3},{1,0},{2,1},{3,2},{4,7},{5,4},{6,5},{7,6},{8,11},{9,8},{10,9... | collective-permute-start | bytes 884744 | tf_op jit(solution)/shard_map/ppermute | solution.py:38
  90.7 15.2 %collective-permute-start.20 = (bf16[288,512]{1,0:T(8,128)(2,1)S(1)}, bf16[288,512]{1,0:T(8,128)(2,1)S(1)}, u32[]{:S(2)}, u32[]{:S(2)}) collective-permute-start(bf16[288,512]{1,0:T(8,128)(2,1)S(1)} %pad_maximum_fusion.3), channel_id=1, source_target_pairs={{0,1},{1,2},{2,3},{3,0},{4,5},{5,6},{6,7},{7,4},{8,9},{9,10},{10,1... | collective-permute-start | bytes 884744 | tf_op jit(solution)/shard_map/ppermute | solution.py:38
  96.6 10.4 %collective-permute-start.16 = (bf16[256,512]{1,0:T(8,128)(2,1)S(1)}, bf16[256,512]{1,0:T(8,128)(2,1)S(1)}, u32[]{:S(2)}, u32[]{:S(2)}) collective-permute-start(bf16[256,512]{1,0:T(8,128)(2,1)S(1)} %pad_maximum_fusion.5), channel_id=1, source_target_pairs={{0,3},{1,0},{2,1},{3,2},{4,7},{5,4},{6,5},{7,6},{8,11},{9,8},{10,9... | collective-permute-start | bytes 786440 | tf_op jit(solution)/shard_map/ppermute | solution.py:38
  98.9 14.4 %collective-permute-start.14 = (bf16[512,512]{1,0:T(8,128)(2,1)S(1)}, bf16[512,512]{1,0:T(8,128)(2,1)S(1)}, u32[]{:S(2)}, u32[]{:S(2)}) collective-permute-start(bf16[512,512]{1,0:T(8,128)(2,1)S(1)} %pad_maximum_fusion), channel_id=1, source_target_pairs={{0,1},{1,2},{2,3},{3,0},{4,5},{5,6},{6,7},{7,4},{8,9},{9,10},{10,1... | collective-permute-start | bytes 1572872 | tf_op jit(solution)/shard_map/ppermute | solution.py:38
  100.2 8.3 %collective-permute-start.28 = (bf16[64,512]{1,0:T(8,128)(2,1)S(1)}, bf16[64,512]{1,0:T(8,128)(2,1)S(1)}, u32[]{:S(2)}, u32[]{:S(2)}) collective-permute-start(bf16[64,512]{1,0:T(8,128)(2,1)S(1)} %add_convert_fusion.8), channel_id=1, source_target_pairs={{0,192},{8,200},{16,208},{24,216},{32,224},{40,232},{48,240},{56,2... | collective-permute-start | bytes 196616 | tf_op jit(solution)/shard_map/ppermute | solution.py:69
  106.1 9.3 %collective-permute-start.23 = (bf16[512,512]{1,0:T(8,128)(2,1)S(1)}, bf16[512,512]{1,0:T(8,128)(2,1)S(1)}, u32[]{:S(2)}, u32[]{:S(2)}) collective-permute-start(bf16[512,512]{1,0:T(8,128)(2,1)S(1)} %pad_maximum_fusion.2), channel_id=1, source_target_pairs={{0,4},{1,5},{2,6},{3,7},{4,0},{5,1},{6,2},{7,3},{8,12},{9,13},{10,... | collective-permute-start | bytes 1572872 | tf_op jit(solution)/shard_map/ppermute | solution.py:42
  107.2 10.5 %collective-permute-start.18 = (bf16[512,512]{1,0:T(8,128)(2,1)S(1)}, bf16[512,512]{1,0:T(8,128)(2,1)S(1)}, u32[]{:S(2)}, u32[]{:S(2)}) collective-permute-start(bf16[512,512]{1,0:T(8,128)(2,1)S(1)} %pad_maximum_fusion.1), channel_id=1, source_target_pairs={{0,3},{1,0},{2,1},{3,2},{4,7},{5,4},{6,5},{7,6},{8,11},{9,8},{10,9... | collective-permute-start | bytes 1572872 | tf_op jit(solution)/shard_map/ppermute | solution.py:38
  (34 other events, 263.4 us)

commit v2 on v0

v2 whole, which is shorter than its diff:
```python
import functools

import jax
import jax.numpy as jnp
from jax import lax
from jax.experimental import pallas as pl
from jax.experimental.pallas import tpu as pltpu
from jax.sharding import PartitionSpec as P

DW = 4096
HV = 512
SLAB = 512
TOK = 512
NFRAG = 4
FRAG = SLAB // NFRAG
N_REP = 32
HALF = SLAB // 2
PART = HALF // 2
LOWER = 288
UPPER = SLAB - LOWER
SOME = LOWER // 2
ORDER = (6, 2, 3, 5, 7, 4, 1, 0)
AT = {shard: i for i, shard in enumerate(ORDER)}

INNER_RATE = 0.05
INNER_BETA = 0.9
OUTER_RATE = 0.7
OUTER_BETA = 0.9
MIX_SHARE = 0.5
SCALE = DW ** (-0.5)

F32 = jnp.float32
BF16 = jnp.bfloat16
MIB = 1024 * 1024
LIMIT = 16 * MIB
HINT = pl.CostEstimate(flops=1024, bytes_accessed=1024, transcendentals=0)


def move_y(value, step):
    pairs = [(z * 4 + y, z * 4 + (y + step) % 4) for z in range(2) for y in range(4)]
    return lax.ppermute(value, "fsdp", pairs)


def move_z(value):
    return lax.ppermute(value, "fsdp", [(i, (i + 4) % 8) for i in range(8)])


def swap_core(value):
    return lax.ppermute(value, "rep", [(i, i ^ 1) for i in range(32)])


def swap_x(value, flip):
    pairs = []
    for i in range(32):
        x = (i // 2) % 4
        pairs.append((i, i + 2 * ((x ^ flip) - x)))
    return lax.ppermute(value, "rep", pairs)


def swap_z(value, flip):
    pairs = []
    for i in range(32):
        h = i // 8
        pairs.append((i, i + 8 * ((h ^ flip) - h)))
    return lax.ppermute(value, "rep", pairs)


HBM = pl.BlockSpec(memory_space=pl.ANY)
SMEM = pl.BlockSpec(memory_space=pltpu.SMEM)
VMEM = pl.BlockSpec(memory_space=pltpu.VMEM)


def add16(*terms):
    total = terms[0].astype(F32)
    for term in terms[1:]:
        total = total + term.astype(F32)
    return total


def add_rounded(*terms):
    return add16(*terms).astype(BF16)


def start_all(pairs, sems, at=0):
    copies = []
    for i, (source, target) in enumerate(pairs):
        copy = pltpu.make_async_copy(source, target, sems.at[at + i])
        copy.start()
        copies.append(copy)
    return copies


def wait_all(copies):
    for copy in copies:
        copy.wait()


def local_call(kernel, near_outs, far_outs, scratch, scalars=(), near=(), far=(), late=(), aliases=None):
    outs = tuple(pltpu.VMEM(s, t) for s, t in near_outs)
    outs += tuple(pltpu.HBM(s, t) for s, t in far_outs)
    count = len(scalars) + len(near) + len(far)

    def run(*refs):
        kernel(*refs[:count], *refs[count + len(late) :])

    held = [pltpu.with_memory_space_constraint(a, pltpu.VMEM) for a in near]
    held += [pltpu.with_memory_space_constraint(a, pltpu.HBM) for a in far]
    held += [pltpu.with_memory_space_constraint(a, pltpu.HBM if in_hbm else pltpu.VMEM) for a, in_hbm in late]
    return pl.pallas_call(
        run,
        out_shape=outs,
        in_specs=[SMEM] * len(scalars) + [VMEM] * len(near) + [HBM] * (len(far) + len(late)),
        out_specs=(VMEM,) * len(near_outs) + (HBM,) * len(far_outs),
        scratch_shapes=scratch,
        input_output_aliases=aliases or {},
        compiler_params=pltpu.CompilerParams(vmem_limit_bytes=LIMIT),
        cost_estimate=HINT,
    )(*scalars, *held)


def rows16(rows):
    return ((rows, HV), BF16)


def slab_columns(where, shard):
    me = where[0]
    place = ((me // 4 + shard // 4) % 2) * 4 + (me % 4 + shard % 4) % 4
    return pl.ds(pl.multiple_of(place * SLAB, SLAB), SLAB)


def first_kernel(weights, w, w_lo, w_hi, held, sems):
    loads = [(weights.at[pl.ds(i * FRAG, FRAG)], held.at[pl.ds(i * FRAG, FRAG)]) for i in range(NFRAG)]
    for i, load in enumerate(start_all(loads, sems)):
        load.wait()
        part = held[i * FRAG : (i + 1) * FRAG].astype(BF16)
        w[i * FRAG : (i + 1) * FRAG] = part
        target, at = (w_lo, i * FRAG) if i < NFRAG // 2 else (w_hi, i * FRAG - HALF)
        target[at : at + FRAG] = part


def first(weights):
    scratch = [pltpu.VMEM((SLAB, HV), F32), pltpu.SemaphoreType.DMA((NFRAG,))]
    outs = [rows16(SLAB), rows16(HALF), rows16(HALF)]
    return local_call(first_kernel, outs, [], scratch, far=[weights])


def leaving_kernel(where, plan, weights, outer, mine, theirs, held, theta, sems):
    rows = pl.ds(pl.multiple_of(plan[2] * FRAG, FRAG), FRAG)
    wait_all(start_all([(weights.at[rows], held), (outer.at[rows], theta)], sems))
    theta[...] = theta[...] - held[...]
    half = FRAG // 2
    mine[...] = theta[pl.ds(pl.multiple_of(where[1] * half, half), half), :].astype(BF16)
    theirs[...] = theta[pl.ds(pl.multiple_of((1 - where[1]) * half, half), half), :].astype(BF16)


def leaving(where, plan, weights, outer, late):
    scratch = [pltpu.VMEM((FRAG, HV), F32), pltpu.VMEM((FRAG, HV), F32), pltpu.SemaphoreType.DMA((2,))]
    outs = [rows16(FRAG // 2)] * 2
    return local_call(leaving_kernel, outs, [], scratch, [where, plan], [], [weights, outer], late)


def turn_kernel(where, x, target, slabs, turned, goal, sems):
    loads = start_all([(x.at[:, slab_columns(where, d)], slabs.at[i]) for i, d in enumerate(ORDER)], sems)
    last = start_all([(target, goal)], sems, 8)
    for d in range(8):
        loads[d].wait()
        turned[d] = slabs[d].T
    wait_all(last)


def turn(where, activations, target, late):
    return local_call(
        turn_kernel,
        [((8, TOK, SLAB), BF16), ((8, SLAB, TOK), BF16), rows16(TOK)],
        [],
        [pltpu.SemaphoreType.DMA((9,))],
        [where],
        [],
        [activations, target],
        late,
    )


def share_kernel(mine, other, share):
    share[...] = add_rounded(mine[...], other[...])


def add_share(mine, other, late=()):
    return local_call(share_kernel, [rows16(FRAG // 2)], [], [], near=[mine, other], late=late)[0]


def share_first_kernel(held, mine, other, same, share):
    share[...] = add_rounded(mine[...], other[...])


def second_kernel(w_lo, w_hi, back_hi, next_hi, z_lo, mine, other, to_next, to_back, to_z, share):
    to_next[:HALF] = z_lo[...]
    to_next[HALF:] = back_hi[...]
    to_back[:HALF] = z_lo[...]
    to_back[HALF:] = w_lo[...]
    to_z[:HALF] = w_hi[...]
    to_z[HALF : 2 * HALF] = next_hi[...]
    to_z[2 * HALF :] = back_hi[...]
    share[...] = add_rounded(mine[...], other[...])


def third_kernel(w_lo, y_back, y_next, mine, other, to_next, to_back, to_z, share):
    to_next[:PART] = y_back[PART:HALF]
    to_next[PART:] = w_lo[...]
    to_back[:PART] = y_next[:PART]
    to_back[PART:] = y_next[HALF:]
    to_z[...] = y_back[HALF:]
    share[...] = add_rounded(mine[...], other[...])


def parts_of(parts, sources):
    values = [sources[source][at : at + rows] for source, at, rows in parts]
    return values[0] if len(values) == 1 else jnp.concatenate(values, axis=0)


def value_terms(table, slabs, sources):
    for shard, row, parts in table:
        weights = parts_of(parts, sources)
        columns = slabs[AT[shard], :, row : row + weights.shape[0]]
        yield jnp.dot(columns, weights, preferred_element_type=F32)


def forward_kernel(table, slabs, *refs):
    *sources, out = refs
    for j, term in enumerate(value_terms(table, slabs, sources)):
        out[...] = term if j == 0 else out[...] + term


def forward(slabs, sources, table, late):
    kernel = functools.partial(forward_kernel, table)
    return local_call(kernel, [((TOK, HV), F32)], [], [], near=[slabs, *sources], late=late)[0]


def middle_kernel(table, slabs, turned, before, target, y_back, y_next, z_far, *outs):
    cot, to_next, to_back, to_z, p02_hi, p03_hi = outs
    total = before[...]
    for term in value_terms(table, slabs, (y_back, y_next, z_far)):
        total = total + term
    cot[...] = (total * SCALE - target[...].astype(F32)).astype(BF16)
    p12, p02, p03 = (
        jnp.dot(turned[d], cot[...], preferred_element_type=F32).astype(BF16) for d in range(3)
    )
    to_next[:SOME] = p12[:SOME]
    to_next[SOME:] = p02[:LOWER]
    to_back[:SOME] = p12[SOME:LOWER]
    to_back[SOME:] = p03[:LOWER]
    to_z[...] = p12[LOWER:]
    p02_hi[...] = p02[LOWER:]
    p03_hi[...] = p03[LOWER:]


def middle(slabs, turned, before, target, sources, table):
    three = [rows16(SOME + LOWER), rows16(SOME + LOWER), rows16(UPPER)]
    return local_call(
        functools.partial(middle_kernel, table),
        [rows16(TOK)] + three + [rows16(UPPER)] * 2,
        [],
        [],
        near=[slabs, turned, before, target, *sources],
    )


def backward_kernel(turned, cot, p11_lo, p13_lo, p10_lo, to_z, p01, p00):
    for i, low in enumerate((p11_lo, p13_lo, p10_lo)):
        part = jnp.dot(turned[3 + i], cot[...], preferred_element_type=F32).astype(BF16)
        low[...] = part[:LOWER]
        to_z[i * UPPER : (i + 1) * UPPER] = part[LOWER:]
    p01[...] = jnp.dot(turned[6], cot[...], preferred_element_type=F32).astype(BF16)
    p00[...] = jnp.dot(turned[7], cot[...], preferred_element_type=F32).astype(BF16)


def input_kernel(table, where, cot, *refs):
    *sources, out, products, sems = refs
    stores = []
    for j, (shard, parts) in enumerate(table):
        product = lax.dot_general(
            cot[...],
            parts_of(parts, sources),
            (((1,), (1,)), ((), ())),
            preferred_element_type=F32,
        )
        products[j] = (product * SCALE).astype(BF16)
        stores += start_all([(products.at[j], out.at[:, slab_columns(where, shard)])], sems, j)
    wait_all(stores)


def input_gradient(where, cotangent, sources, table, late):
    by_shard = [(d, sum([p for s, _, p in sorted(table, key=lambda t: t[1]) if s == d], [])) for d in ORDER[::-1]]
    return local_call(
        functools.partial(input_kernel, by_shard),
        [],
        [((TOK, DW), BF16)],
        [pltpu.VMEM((8, TOK, SLAB), BF16), pltpu.SemaphoreType.DMA((8,))],
        [where],
        [cotangent, *sources],
        [],
        late,
    )[0]


def join_second_kernel(
    p11_lo, p13_lo, p01, p02_hi, from_back, from_next, in02_hi, to_next, to_back
):
    to_next[:SOME] = add_rounded(p11_lo[:SOME], from_back[:SOME])
    to_next[SOME:LOWER] = p11_lo[SOME:]
    to_next[LOWER:] = add_rounded(p01[:LOWER], from_back[SOME:])
    to_back[:SOME] = p13_lo[:SOME]
    to_back[SOME:LOWER] = add_rounded(p13_lo[SOME:], from_next[:SOME])
    to_back[LOWER:] = add_rounded(p02_hi[...], in02_hi[...])


def join_third_kernel(
    p01, p03_hi, p10_lo, from_back, from_next, in_hi, mine, other, to_next, to_back, to_z, share
):
    to_next[...] = add_rounded(p01[LOWER:], in_hi[:UPPER])
    to_back[...] = add_rounded(p03_hi[...], in_hi[UPPER : 2 * UPPER], from_next[LOWER:])
    to_z[...] = add_rounded(p10_lo[...], from_back[:LOWER], from_next[:LOWER])
    share[...] = add_rounded(mine[...], other[...])


def outer_kernel(plan, outer, moment, pending, params, inner, late, old, speed, new_outer, new_moment, held, push, came, sems):
    loads = start_all(
        [(outer, held), (moment, push), (pending, came), (params, old), (inner, speed)], sems
    )
    wait_all(loads[:3])
    rows = pl.ds(pl.multiple_of(plan[0] * FRAG, FRAG), FRAG)
    arrived = came[...]
    moment_late = OUTER_BETA * push[rows, :] + arrived
    outer_late = held[rows, :] - OUTER_RATE * (arrived + OUTER_BETA * moment_late)
    push[rows, :] = moment_late
    held[rows, :] = outer_late
    late[...] = outer_late
    stores = start_all([(held, new_outer), (push, new_moment)], sems, 5)
    wait_all(loads[3:] + stores)


def outer_step(plan, outer, moment, pending, params, inner, late):
    return local_call(
        outer_kernel,
        [((FRAG, HV), F32), ((SLAB, HV), F32), ((SLAB, HV), F32)],
        [((SLAB, HV), F32)] * 2,
        [
            pltpu.VMEM((SLAB, HV), F32),
            pltpu.VMEM((SLAB, HV), F32),
            pltpu.VMEM((FRAG, HV), F32),
            pltpu.SemaphoreType.DMA((7,)),
        ],
        [plan],
        [],
        [outer, moment, pending, params, inner],
        late,
    )


def step_kernel(where, plan, late, old, speed, share, other, own, low1, low2, low3, high1, high2, high3, *refs):
    new_params, new_moment, new_pending, params, moment, mean, sems = refs
    terms = [(low1, SOME), (low2, LOWER), (low3, 0)], [(high1, 2 * UPPER), (high2, 0), (high3, 0)]
    half = FRAG // 2
    mean[pl.ds(pl.multiple_of(where[1] * half, half), half), :] = share[...].astype(F32) / N_REP
    mean[pl.ds(pl.multiple_of((1 - where[1]) * half, half), half), :] = other[...].astype(F32) / N_REP
    stores = start_all([(mean, new_pending)], sems, 2 * NFRAG)
    for i in range(NFRAG):
        rows = pl.ds(i * FRAG, FRAG)
        first, end = i * FRAG, (i + 1) * FRAG
        cuts = [(0, first, min(end, LOWER)), (1, max(first, LOWER), end)]
        others = []
        for part, begin, stop in cuts:
            if begin < stop:
                at = begin - part * LOWER
                others.append(add16(*[t[row + at : row + at + stop - begin] for t, row in terms[part]]))
        others = others[0] if len(others) == 1 else jnp.concatenate(others, axis=0)
        fresh = INNER_BETA * speed[rows, :] + add16(own[rows, :], others) * SCALE
        moment[rows, :] = fresh
        stores += start_all([(moment.at[rows], new_moment.at[rows])], sems, 2 * i)
        stepped = old[rows, :] - INNER_RATE * fresh
        merged = MIX_SHARE * stepped + MIX_SHARE * late[...]
        params[rows, :] = jnp.where(plan[0] == i, merged, stepped)
        stores += start_all([(params.at[rows], new_params.at[rows])], sems, 2 * i + 1)
    wait_all(stores)


def inner_step(where, plan, near):
    return local_call(
        step_kernel,
        [],
        [((SLAB, HV), F32), ((SLAB, HV), F32), ((FRAG, HV), F32)],
        [
            pltpu.VMEM((SLAB, HV), F32),
            pltpu.VMEM((SLAB, HV), F32),
            pltpu.VMEM((FRAG, HV), F32),
            pltpu.SemaphoreType.DMA((2 * NFRAG + 1,)),
        ],
        [where, plan],
        near,
    )


def body(activations, target, params, momentum, outer_params, outer_momentum, pending, plan):
    weights, moment = params[0], momentum[0]
    where = jnp.stack([lax.axis_index("fsdp"), lax.axis_index("rep") % 2]).astype(jnp.int32)
    share_rows = rows16(FRAG // 2)

    w, w_lo, w_hi = first(weights)
    z_lo, back_hi, next_hi = move_z(w_lo), move_y(w_hi, 1), move_y(w_hi, -1)
    mine, theirs = leaving(where, plan, weights, outer_params, [(w, False)])
    other = swap_core(theirs)

    to_next, to_back, to_z, share = local_call(
        second_kernel,
        [rows16(2 * HALF), rows16(2 * HALF), rows16(3 * HALF), share_rows],
        [],
        [],
        near=[w_lo, w_hi, back_hi, next_hi, z_lo, mine, other],
    )
    z_hi, y_back, y_next = move_z(to_z), move_y(to_next, 1), move_y(to_back, -1)
    slabs, turned, goal = turn(where, activations, target, [(share, False)])
    share = add_share(share, swap_x(share, 1))
    other = swap_x(share, 3)

    to_next, to_back, to_z, share = local_call(
        third_kernel,
        [rows16(PART + HALF), rows16(PART + HALF), rows16(HALF), share_rows],
        [],
        [],
        near=[w_lo, y_back, y_next, share, other],
        late=[(goal, False)],
    )
    z_far, y_back3, y_next3 = move_z(to_z), move_y(to_next, 1), move_y(to_back, -1)
    other = swap_z(share, 1)

    near = [w, next_hi, back_hi, z_lo, y_back, y_next, z_hi]
    upper = SLAB - HALF
    table = [
        (0, 0, [(0, 0, SLAB)]),
        (1, 0, [(5, HALF, HALF), (1, 0, upper)]),
        (4, 0, [(3, 0, HALF), (6, 0, upper)]),
        (5, 0, [(5, 0, HALF), (6, HALF, upper)]),
        (7, 0, [(4, 0, HALF), (6, 2 * HALF, upper)]),
        (3, HALF, [(2, 0, upper)]),
        (2, HALF, [(4, HALF, upper)]),
    ]
    late, old, speed, new_outer, new_outer_momentum = outer_step(
        plan, outer_params, outer_momentum, pending, weights, moment, [(to_z, False)]
    )
    values = forward(slabs, near, table, [(late, False)])
    last = [y_back3, y_next3, z_far]
    cotangent, to_next, to_back, to_z, p02_hi, p03_hi = middle(
        slabs,
        turned,
        values,
        goal,
        last,
        [
            (3, 0, [(0, PART, HALF)]),
            (2, 0, [(1, PART, HALF)]),
            (6, 0, [(1, 0, PART), (0, 0, PART), (2, 0, upper)]),
        ],
    )

    in02_hi, from_back, from_next = move_z(to_z), move_y(to_next, 1), move_y(to_back, -1)
    low1 = from_next
    p11_lo, p13_lo, p10_lo, to_z, p01, p00 = local_call(
        backward_kernel,
        [rows16(LOWER)] * 3 + [rows16(3 * UPPER), rows16(SLAB), rows16(SLAB)],
        [],
        [],
        near=[turned, cotangent],
    )
    to_z, share = local_call(
        share_first_kernel,
        [rows16(3 * UPPER), share_rows],
        [],
        [],
        near=[to_z, share, other],
        aliases={0: 0},
    )
    in_hi = move_z(to_z)

    to_next, to_back = local_call(
        join_second_kernel,
        [rows16(2 * LOWER), rows16(SLAB)],
        [],
        [],
        near=[p11_lo, p13_lo, p01, p02_hi, from_back, from_next, in02_hi],
    )
    from_back, from_next = move_y(to_next, 1), move_y(to_back, -1)
    low2 = from_back
    other = swap_z(share, 3)
    table += [
        (3, 0, [(7, PART, HALF)]),
        (2, 0, [(8, PART, HALF)]),
        (6, 0, [(8, 0, PART), (7, 0, PART), (9, 0, upper)]),
    ]
    grad_input = input_gradient(where, cotangent, near + last, table, [(to_back, False)])

    to_next, to_back, to_z, share = local_call(
        join_third_kernel,
        [rows16(UPPER), rows16(UPPER), rows16(LOWER), share_rows],
        [],
        [],
        near=[p01, p03_hi, p10_lo, from_back, from_next, in_hi, share, other],
        late=[(grad_input, True)],
    )
    low3, high2, high3 = move_z(to_z), move_y(to_next, 1), move_y(to_back, -1)
    other = swap_core(share)

    terms = [p00, low1, low2, low3, in_hi, high2, high3]
    new_params, new_moment, new_pending = inner_step(
        where, plan, [late, old, speed, share, other, *terms]
    )
    return (
        new_params[None],
        new_moment[None],
        grad_input,
        new_outer,
        new_outer_momentum,
        new_pending,
    )


def solution(mesh):
    placed = (
        P(("rep", "fsdp"), None),
        P(("rep", "fsdp"), None),
        P("rep", "fsdp", None),
        P("rep", "fsdp", None),
        P("fsdp", None),
        P("fsdp", None),
        P("fsdp", None),
        P(),
    )
    return jax.shard_map(
        body,
        mesh=mesh,
        in_specs=placed,
        out_specs=(
            P("rep", "fsdp", None),
            P("rep", "fsdp", None),
            P(("rep", "fsdp"), None),
            P("fsdp", None),
            P("fsdp", None),
            P("fsdp", None),
        ),
        check_vma=False,
    )
```

time: 409 us -> 85.5 us (0.21)
  waiting for transfers between devices: 361 us -> 22.8 us
  starting transfers between devices: 0.12 us -> 39.7 us
  Pallas kernels: 0 us -> 21.1 us
  matrix products: 17.5 us -> 0 us
  between operations: 17.7 us -> 0.96 us
  other arithmetic: 6.89 us -> 0.07 us
    psum x1 -> x0, waiting for transfers between devices: 257 us -> none  [body(): lax.psum(pseudo_grad.astype(jnp.bfloat16), 'rep').astype(jnp.float32)]
    all_gather x1 -> x0, waiting for transfers between devices: 55.8 us -> none  [body(): gathered = lax.all_gather(weights16, 'fsdp', axis=0, tiled=True)]
    reduce_scatter x1 -> x0, waiting for transfers between devices: 48.8 us -> none  [body(): lax.psum_scatter(lax.dot_general(activations, cotangent, (((0,), (0,)), (...]
    ppermute x0 -> x24, starting transfers between devices: none -> 39.7 us  [the longest x12 16.8 us: move_y(): return lax.ppermute(value, 'fsdp', pairs)]
    ppermute x0 -> x24, waiting for transfers between devices: none -> 22.8 us  [the longest x2 9.26 us: swap_z(): return lax.ppermute(value, 'rep', pairs)]
    pallas_call x0 -> x15, Pallas kernels: none -> 21.1 us  [local_call(): pl.pallas_call(run, out_shape=outs, in_specs=[SMEM] * len(scalars) + [VME...]
    dot_general x3 -> x0, matrix products: 17.5 us -> none  [the longest x1 7.11 us: body(): lax.dot_general(cotangent, gathered, (((1,), (1,)), ((), ())), preferred_...]
  transfers between devices with their start and end apart: 3 -> 24, of which waited for: 3 -> 11; matrix products, arithmetic and copies ran while one was open for 2% -> 0% of each run, Pallas kernels for 0% -> 19%
where the time goes in v2:
time: 85.5 us; the launch traced here: 85.3 us
  starting transfers between devices  39.7 us (46%)
  waiting for transfers between devices  22.8 us (27%)
  Pallas kernels  21.1 us (25%)
  between operations  0.96 us (1%)
    pallas_call x15, Pallas kernels, local_call(): pl.pallas_call(run, out_shape=outs, in_specs=[SMEM] * len(scalars) + [VME...  21.1 us
    ppermute x12, starting transfers between devices, move_y(): return lax.ppermute(value, 'fsdp', pairs)  16.8 us
    ppermute x6, starting transfers between devices, move_z(): return lax.ppermute(value, 'fsdp', [(i, (i + 4) % 8) for i in range(8)])  12.6 us
    ppermute x2, waiting for transfers between devices, swap_z(): return lax.ppermute(value, 'rep', pairs)  9.26 us
    ppermute x12, waiting for transfers between devices, move_y(): return lax.ppermute(value, 'fsdp', pairs)  8.09 us
    ppermute x2, starting transfers between devices, swap_z(): return lax.ppermute(value, 'rep', pairs)  5.93 us
    ppermute x2, starting transfers between devices, swap_x(): return lax.ppermute(value, 'rep', pairs)  4.34 us
    ppermute x2, waiting for transfers between devices, swap_x(): return lax.ppermute(value, 'rep', pairs)  2.78 us
  transfers between devices with their start and end apart: 24, of which 11 were waited for; matrix products, arithmetic and copies ran while one was open for 0% of the time, Pallas kernels for 19%

profile of v2, /device:TPU:24, one launch (start us, length us, event | category | flops | bytes accessed | tf_op | source)
XLA Modules:
  0.0 85.3 jit_solution(9549467721472799815)
XLA Ops:
  1.9 2.0 %collective-permute-start = (bf16[256,512]{1,0:T(8,128)(2,1)S(1)}, bf16[256,512]{1,0:T(8,128)(2,1)S(1)}, u32[]{:S(2)}, u32[]{:S(2)}) collective-permute-start(bf16[256,512]{1,0:T(8,128)(2,1)S(1)} %get-tuple-element.51.refs_1_), channel_id=1, source_target_pairs={{0,1},{1,2},{2,3},{3,0},{4,5},{5,6},{6,7},{7,4},{8,9},{9,10},{10,1... | collective-permute-start | bytes 786440 | tf_op jit(solution)/shard_map/ppermute | solution.py:41
  4.0 1.9 %collective-permute-start.2 = (bf16[256,512]{1,0:T(8,128)(2,1)S(1)}, bf16[256,512]{1,0:T(8,128)(2,1)S(1)}, u32[]{:S(2)}, u32[]{:S(2)}) collective-permute-start(bf16[256,512]{1,0:T(8,128)(2,1)S(1)} %get-tuple-element.50.refs_0_), channel_id=1, source_target_pairs={{0,4},{1,5},{2,6},{3,7},{4,0},{5,1},{6,2},{7,3},{8,12},{9,13},{10,... | collective-permute-start | bytes 786440 | tf_op jit(solution)/shard_map/ppermute | solution.py:45
  11.8 2.0 %collective-permute-start.4 = (bf16[512,512]{1,0:T(8,128)(2,1)S(1)}, bf16[512,512]{1,0:T(8,128)(2,1)S(1)}, u32[]{:S(2)}, u32[]{:S(2)}) collective-permute-start(bf16[512,512]{1,0:T(8,128)(2,1)S(1)} %get-tuple-element.55), channel_id=1, source_target_pairs={{0,1},{1,2},{2,3},{3,0},{4,5},{5,6},{6,7},{7,4},{8,9},{9,10},{10,1... | collective-permute-start | bytes 1572872 | tf_op jit(solution)/shard_map/ppermute | solution.py:41
  13.9 1.7 %collective-permute-start.8 = (bf16[768,512]{1,0:T(8,128)(2,1)S(1)}, bf16[768,512]{1,0:T(8,128)(2,1)S(1)}, u32[]{:S(2)}, u32[]{:S(2)}) collective-permute-start(bf16[768,512]{1,0:T(8,128)(2,1)S(1)} %get-tuple-element.65), channel_id=1, source_target_pairs={{0,4},{1,5},{2,6},{3,7},{4,0},{5,1},{6,2},{7,3},{8,12},{9,13},{10,... | collective-permute-start | bytes 2359304 | tf_op jit(solution)/shard_map/ppermute | solution.py:45
  17.1 2.8 %collective-permute-done.6.refs_1_ = bf16[64,512]{1,0:T(8,128)(2,1)S(1)} collective-permute-done((bf16[64,512]{1,0:T(8,128)(2,1)S(1)}, bf16[64,512]{1,0:T(8,128)(2,1)S(1)}, u32[]{:S(2)}, u32[]{:S(2)}) %collective-permute-start.6) | collective-permute-done | bytes 65568 | tf_op jit(solution)/shard_map/ppermute | solution.py:57
  19.9 2.8 %collective-permute-start.7 = (bf16[64,512]{1,0:T(8,128)(2,1)S(1)}, bf16[64,512]{1,0:T(8,128)(2,1)S(1)}, u32[]{:S(2)}, u32[]{:S(2)}) collective-permute-start(bf16[64,512]{1,0:T(8,128)(2,1)S(1)} %shard_map.130.refs_3_), channel_id=1, source_target_pairs={{0,48},{8,56},{16,32},{24,40},{32,16},{40,24},{48,0},{56,8},{64,11... | collective-permute-start | bytes 196616 | tf_op jit(solution)/shard_map/ppermute | solution.py:57
  22.8 3.2 %shard_map.131 = (bf16[8,512,512]{2,1,0:T(8,128)(2,1)S(1)}, bf16[8,512,512]{2,1,0:T(8,128)(2,1)S(1)}, bf16[512,512]{1,0:T(8,128)(2,1)S(1)}) custom-call(s32[2]{0:T(128)S(1)} %pad_add_fusion.refs_0_, bf16[512,4096]{1,0:T(8,128)(2,1)} %refs_1_.5, bf16[512,512]{1,0:T(8,128)(2,1)} %refs_2_.2, bf16[64,512]{1,0:T(8,128)(2,1)S(1)} %get-tuple-element.57.refs_0_.refs_3_), custom_call_target="tpu_custom_call" | custom-call | flops 1024 | bytes 1024 | tf_op jit(solution)/shard_map/pallas_call | solution.py:109
  26.9 2.7 %collective-permute-start.9 = (bf16[384,512]{1,0:T(8,128)(2,1)S(1)}, bf16[384,512]{1,0:T(8,128)(2,1)S(1)}, u32[]{:S(2)}, u32[]{:S(2)}) collective-permute-start(bf16[384,512]{1,0:T(8,128)(2,1)S(1)} %get-tuple-element.66), channel_id=1, source_target_pairs={{0,1},{1,2},{2,3},{3,0},{4,5},{5,6},{6,7},{7,4},{8,9},{9,10},{10,1... | collective-permute-start | bytes 1179656 | tf_op jit(solution)/shard_map/ppermute | solution.py:41
  29.6 2.2 %collective-permute-start.11 = (bf16[256,512]{1,0:T(8,128)(2,1)S(1)}, bf16[256,512]{1,0:T(8,128)(2,1)S(1)}, u32[]{:S(2)}, u32[]{:S(2)}) collective-permute-start(bf16[256,512]{1,0:T(8,128)(2,1)S(1)} %get-tuple-element.59.refs_6_), channel_id=1, source_target_pairs={{0,4},{1,5},{2,6},{3,7},{4,0},{5,1},{6,2},{7,3},{8,12},{9,13},{10,... | collective-permute-start | bytes 786440 | tf_op jit(solution)/shard_map/ppermute | solution.py:45
  31.8 3.6 %shard_map.133 = (f32[128,512]{1,0:T(8,128)S(1)}, f32[512,512]{1,0:T(8,128)S(1)}, f32[512,512]{1,0:T(8,128)S(1)}, f32[512,512]{1,0:T(8,128)}, f32[512,512]{1,0:T(8,128)}) custom-call(s32[4]{0:T(128)S(1)} %copy-done.1, f32[512,512]{1,0:T(8,128)} %refs_1_.6, f32[512,512]{1,0:T(8,128)} %refs_2_.3, f32[128,512]{1,0:T(8,128)} %refs_3_.3, f32[512,512]{1,0:T(8,128)} %bitcast.8, ...), custom_call_target="tpu_custom_call" | custom-call | flops 1024 | bytes 1024 | tf_op jit(solution)/shard_map/pallas_call | solution.py:109
  35.4 1.8 %shard_map.134.refs_2_ = f32[512,512]{1,0:T(8,128)S(1)} custom-call(bf16[8,512,512]{2,1,0:T(8,128)(2,1)S(1)} %get-tuple-element.64.refs_0_, bf16[512,512]{1,0:T(8,128)(2,1)S(1)} %get-tuple-element.52.refs_4_.refs_1_.refs_2_, bf16[256,512]{1,0:T(8,128)(2,1)S(1)} %collective-permute-done.1.refs_3_.refs_2_, ...), custom_call_target="tpu_custom_call" | custom-call | flops 1024 | bytes 1024 | tf_op jit(solution)/shard_map/pallas_call | solution.py:109
  37.2 1.6 %shard_map.135 = (bf16[512,512]{1,0:T(8,128)(2,1)S(1)}, bf16[432,512]{1,0:T(8,128)(2,1)S(1)}, bf16[432,512]{1,0:T(8,128)(2,1)S(1)}, bf16[224,512]{1,0:T(8,128)(2...) custom-call(bf16[8,512,512]{2,1,0:T(8,128)(2,1)S(1)} %get-tuple-element.64.refs_0_, ...), custom_call_target="tpu_custom_call" | custom-call | flops 1024 | bytes 1024 | tf_op jit(solution)/shard_map/pallas_call | solution.py:109
  38.9 2.7 %collective-permute-start.12 = (bf16[432,512]{1,0:T(8,128)(2,1)S(1)}, bf16[432,512]{1,0:T(8,128)(2,1)S(1)}, u32[]{:S(2)}, u32[]{:S(2)}) collective-permute-start(bf16[432,512]{1,0:T(8,128)(2,1)S(1)} %get-tuple-element.75), channel_id=1, source_target_pairs={{0,1},{1,2},{2,3},{3,0},{4,5},{5,6},{6,7},{7,4},{8,9},{9,10},{10,1... | collective-permute-start | bytes 1327112 | tf_op jit(solution)/shard_map/ppermute | solution.py:41
  41.6 1.7 %collective-permute-start.14 = (bf16[224,512]{1,0:T(8,128)(2,1)S(1)}, bf16[224,512]{1,0:T(8,128)(2,1)S(1)}, u32[]{:S(2)}, u32[]{:S(2)}) collective-permute-start(bf16[224,512]{1,0:T(8,128)(2,1)S(1)} %get-tuple-element.77), channel_id=1, source_target_pairs={{0,4},{1,5},{2,6},{3,7},{4,0},{5,1},{6,2},{7,3},{8,12},{9,13},{10,... | collective-permute-start | bytes 688136 | tf_op jit(solution)/shard_map/ppermute | solution.py:45
  43.3 3.3 %collective-permute-start.17 = (bf16[64,512]{1,0:T(8,128)(2,1)S(1)}, bf16[64,512]{1,0:T(8,128)(2,1)S(1)}, u32[]{:S(2)}, u32[]{:S(2)}) collective-permute-start(bf16[64,512]{1,0:T(8,128)(2,1)S(1)} %get-tuple-element.81.refs_1_), channel_id=1, source_target_pairs={{0,64},{8,72},{16,80},{24,88},{32,96},{40,104},{48,112},{56,120},{... | collective-permute-start | bytes 196616 | tf_op jit(solution)/shard_map/ppermute | solution.py:65
  49.0 4.8 %collective-permute-start.18 = (bf16[672,512]{1,0:T(8,128)(2,1)S(1)}, bf16[672,512]{1,0:T(8,128)(2,1)S(1)}, u32[]{:S(2)}, u32[]{:S(2)}) collective-permute-start(bf16[672,512]{1,0:T(8,128)(2,1)S(1)} %get-tuple-element.82), channel_id=1, source_target_pairs={{0,4},{1,5},{2,6},{3,7},{4,0},{5,1},{6,2},{7,3},{8,12},{9,13},{10,... | collective-permute-start | bytes 2064392 | tf_op jit(solution)/shard_map/ppermute | solution.py:45
  54.1 3.3 %collective-permute-start.15 = (bf16[576,512]{1,0:T(8,128)(2,1)S(1)}, bf16[576,512]{1,0:T(8,128)(2,1)S(1)}, u32[]{:S(2)}, u32[]{:S(2)}) collective-permute-start(bf16[576,512]{1,0:T(8,128)(2,1)S(1)} %get-tuple-element.78), channel_id=1, source_target_pairs={{0,1},{1,2},{2,3},{3,0},{4,5},{5,6},{6,7},{7,4},{8,9},{9,10},{10,1... | collective-permute-start | bytes 1769480 | tf_op jit(solution)/shard_map/ppermute | solution.py:41
  57.4 2.7 %collective-permute-start.19 = (bf16[64,512]{1,0:T(8,128)(2,1)S(1)}, bf16[64,512]{1,0:T(8,128)(2,1)S(1)}, u32[]{:S(2)}, u32[]{:S(2)}) collective-permute-start(bf16[64,512]{1,0:T(8,128)(2,1)S(1)} %get-tuple-element.83.refs_6_), channel_id=1, source_target_pairs={{0,192},{8,200},{16,208},{24,216},{32,224},{40,232},{48,240},{56,2... | collective-permute-start | bytes 196616 | tf_op jit(solution)/shard_map/ppermute | solution.py:65
  60.0 3.8 %shard_map.139.refs_8_ = bf16[512,4096]{1,0:T(8,128)(2,1)} custom-call(s32[2]{0:T(128)S(1)} %pad_add_fusion.refs_0_, bf16[512,512]{1,0:T(8,128)(2,1)S(1)} %get-tuple-element.68.refs_1_, bf16[512,512]{1,0:T(8,128)(2,1)S(1)} %get-tuple-element.52.refs_4_.refs_1_.refs_2_, bf16[256,512]{1,0:T(8,128)(2,1)S(1)} %collective-permute-done.1.refs_3_.refs_2_, ...), custom_call_target="tpu_custom_call" | custom-call | flops 1024 | bytes 1024 | tf_op jit(solution)/shard_map/pallas_call | solution.py:109
  63.8 8.4 %collective-permute-done.19.refs_7_ = bf16[64,512]{1,0:T(8,128)(2,1)S(1)} collective-permute-done((bf16[64,512]{1,0:T(8,128)(2,1)S(1)}, bf16[64,512]{1,0:T(8,128)(2,1)S(1)}, u32[]{:S(2)}, u32[]{:S(2)}) %collective-permute-start.19) | collective-permute-done | bytes 65568 | tf_op jit(solution)/shard_map/ppermute | solution.py:65
  72.6 3.3 %collective-permute-start.22 = (bf16[224,512]{1,0:T(8,128)(2,1)S(1)}, bf16[224,512]{1,0:T(8,128)(2,1)S(1)}, u32[]{:S(2)}, u32[]{:S(2)}) collective-permute-start(bf16[224,512]{1,0:T(8,128)(2,1)S(1)} %get-tuple-element.87), channel_id=1, source_target_pairs={{0,1},{1,2},{2,3},{3,0},{4,5},{5,6},{6,7},{7,4},{8,9},{9,10},{10,1... | collective-permute-start | bytes 688136 | tf_op jit(solution)/shard_map/ppermute | solution.py:41
  77.2 2.3 %collective-permute-done.22.refs_12_ = bf16[224,512]{1,0:T(8,128)(2,1)S(1)} collective-permute-done((bf16[224,512]{1,0:T(8,128)(2,1)S(1)}, bf16[224,512]{1,0:T(8,128)(2,1)S(1)}, u32[]{:S(2)}, u32[]{:S(2)}) %collective-permute-start.22) | collective-permute-done | bytes 229408 | tf_op jit(solution)/shard_map/ppermute | solution.py:41
  79.4 3.7 %collective-permute-done.23.refs_13_ = bf16[224,512]{1,0:T(8,128)(2,1)S(1)} collective-permute-done((bf16[224,512]{1,0:T(8,128)(2,1)S(1)}, bf16[224,512]{1,0:T(8,128)(2,1)S(1)}, u32[]{:S(2)}, u32[]{:S(2)}) %collective-permute-start.23) | collective-permute-done | bytes 229408 | tf_op jit(solution)/shard_map/ppermute | solution.py:41
  83.1 2.0 %shard_map.141 = (f32[512,512]{1,0:T(8,128)}, f32[512,512]{1,0:T(8,128)}, f32[128,512]{1,0:T(8,128)}) custom-call(s32[2]{0:T(128)S(1)} %pad_add_fusion.refs_0_, s32[4]{0:T(128)S(1)} %copy-done.1, f32[128,512]{1,0:T(8,128)S(1)} %get-tuple-element.60.refs_8_.refs_2_, f32[512,512]{1,0:T(8,128)S(1)} %get-tuple-element.61.refs_3_, ...), custom_call_target="tpu_custom_call" | custom-call | flops 1024 | bytes 1024 | tf_op jit(solution)/shard_map/pallas_call | solution.py:109
  (44 shorter events, 14.0 us)
Async XLA Ops:
  1.9 8.1 %collective-permute-start = (bf16[256,512]{1,0:T(8,128)(2,1)S(1)}, bf16[256,512]{1,0:T(8,128)(2,1)S(1)}, u32[]{:S(2)}, u32[]{:S(2)}) collective-permute-start(bf16[256,512]{1,0:T(8,128)(2,1)S(1)} %get-tuple-element.51.refs_1_), channel_id=1, source_target_pairs={{0,1},{1,2},{2,3},{3,0},{4,5},{5,6},{6,7},{7,4},{8,9},{9,10},{10,1... | collective-permute-start | bytes 786440 | tf_op jit(solution)/shard_map/ppermute | solution.py:41
  3.9 7.6 %collective-permute-start.1 = (bf16[256,512]{1,0:T(8,128)(2,1)S(1)}, bf16[256,512]{1,0:T(8,128)(2,1)S(1)}, u32[]{:S(2)}, u32[]{:S(2)}) collective-permute-start(bf16[256,512]{1,0:T(8,128)(2,1)S(1)} %get-tuple-element.51.refs_1_), channel_id=1, source_target_pairs={{0,3},{1,0},{2,1},{3,2},{4,7},{5,4},{6,5},{7,6},{8,11},{9,8},{10,9... | collective-permute-start | bytes 786440 | tf_op jit(solution)/shard_map/ppermute | solution.py:41
  4.0 7.7 %collective-permute-start.2 = (bf16[256,512]{1,0:T(8,128)(2,1)S(1)}, bf16[256,512]{1,0:T(8,128)(2,1)S(1)}, u32[]{:S(2)}, u32[]{:S(2)}) collective-permute-start(bf16[256,512]{1,0:T(8,128)(2,1)S(1)} %get-tuple-element.50.refs_0_), channel_id=1, source_target_pairs={{0,4},{1,5},{2,6},{3,7},{4,0},{5,1},{6,2},{7,3},{8,12},{9,13},{10,... | collective-permute-start | bytes 786440 | tf_op jit(solution)/shard_map/ppermute | solution.py:45
  8.3 1.3 %collective-permute-start.3 = (bf16[64,512]{1,0:T(8,128)(2,1)S(1)}, bf16[64,512]{1,0:T(8,128)(2,1)S(1)}, u32[]{:S(2)}, u32[]{:S(2)}) collective-permute-start(bf16[64,512]{1,0:T(8,128)(2,1)S(1)} %get-tuple-element.54), channel_id=1, source_target_pairs={{0,8},{8,0},{16,24},{24,16},{32,40},{40,32},{48,56},{56,48},{64,72... | collective-permute-start | bytes 196616 | tf_op jit(solution)/shard_map/ppermute | solution.py:49
  11.8 14.2 %collective-permute-start.4 = (bf16[512,512]{1,0:T(8,128)(2,1)S(1)}, bf16[512,512]{1,0:T(8,128)(2,1)S(1)}, u32[]{:S(2)}, u32[]{:S(2)}) collective-permute-start(bf16[512,512]{1,0:T(8,128)(2,1)S(1)} %get-tuple-element.55), channel_id=1, source_target_pairs={{0,1},{1,2},{2,3},{3,0},{4,5},{5,6},{6,7},{7,4},{8,9},{9,10},{10,1... | collective-permute-start | bytes 1572872 | tf_op jit(solution)/shard_map/ppermute | solution.py:41
  13.7 12.5 %collective-permute-start.5 = (bf16[512,512]{1,0:T(8,128)(2,1)S(1)}, bf16[512,512]{1,0:T(8,128)(2,1)S(1)}, u32[]{:S(2)}, u32[]{:S(2)}) collective-permute-start(bf16[512,512]{1,0:T(8,128)(2,1)S(1)} %get-tuple-element.56), channel_id=1, source_target_pairs={{0,3},{1,0},{2,1},{3,2},{4,7},{5,4},{6,5},{7,6},{8,11},{9,8},{10,9... | collective-permute-start | bytes 1572872 | tf_op jit(solution)/shard_map/ppermute | solution.py:41
  13.9 21.5 %collective-permute-start.8 = (bf16[768,512]{1,0:T(8,128)(2,1)S(1)}, bf16[768,512]{1,0:T(8,128)(2,1)S(1)}, u32[]{:S(2)}, u32[]{:S(2)}) collective-permute-start(bf16[768,512]{1,0:T(8,128)(2,1)S(1)} %get-tuple-element.65), channel_id=1, source_target_pairs={{0,4},{1,5},{2,6},{3,7},{4,0},{5,1},{6,2},{7,3},{8,12},{9,13},{10,... | collective-permute-start | bytes 2359304 | tf_op jit(solution)/shard_map/ppermute | solution.py:45
  15.6 4.3 %collective-permute-start.6 = (bf16[64,512]{1,0:T(8,128)(2,1)S(1)}, bf16[64,512]{1,0:T(8,128)(2,1)S(1)}, u32[]{:S(2)}, u32[]{:S(2)}) collective-permute-start(bf16[64,512]{1,0:T(8,128)(2,1)S(1)} %get-tuple-element.57.refs_0_.refs_3_), channel_id=1, source_target_pairs={{0,16},{8,24},{16,0},{24,8},{32,48},{40,56},{48,32},{56,40},{64,80... | collective-permute-start | bytes 196616 | tf_op jit(solution)/shard_map/ppermute | solution.py:57
  19.9 6.1 %collective-permute-start.7 = (bf16[64,512]{1,0:T(8,128)(2,1)S(1)}, bf16[64,512]{1,0:T(8,128)(2,1)S(1)}, u32[]{:S(2)}, u32[]{:S(2)}) collective-permute-start(bf16[64,512]{1,0:T(8,128)(2,1)S(1)} %shard_map.130.refs_3_), channel_id=1, source_target_pairs={{0,48},{8,56},{16,32},{24,40},{32,16},{40,24},{48,0},{56,8},{64,11... | collective-permute-start | bytes 196616 | tf_op jit(solution)/shard_map/ppermute | solution.py:57
  26.3 10.9 %collective-permute-start.10 = (bf16[384,512]{1,0:T(8,128)(2,1)S(1)}, bf16[384,512]{1,0:T(8,128)(2,1)S(1)}, u32[]{:S(2)}, u32[]{:S(2)}) collective-permute-start(bf16[384,512]{1,0:T(8,128)(2,1)S(1)} %get-tuple-element.67), channel_id=1, source_target_pairs={{0,3},{1,0},{2,1},{3,2},{4,7},{5,4},{6,5},{7,6},{8,11},{9,8},{10,9... | collective-permute-start | bytes 1179656 | tf_op jit(solution)/shard_map/ppermute | solution.py:41
  26.9 10.3 %collective-permute-start.9 = (bf16[384,512]{1,0:T(8,128)(2,1)S(1)}, bf16[384,512]{1,0:T(8,128)(2,1)S(1)}, u32[]{:S(2)}, u32[]{:S(2)}) collective-permute-start(bf16[384,512]{1,0:T(8,128)(2,1)S(1)} %get-tuple-element.66), channel_id=1, source_target_pairs={{0,1},{1,2},{2,3},{3,0},{4,5},{5,6},{6,7},{7,4},{8,9},{9,10},{10,1... | collective-permute-start | bytes 1179656 | tf_op jit(solution)/shard_map/ppermute | solution.py:41
  29.6 7.6 %collective-permute-start.11 = (bf16[256,512]{1,0:T(8,128)(2,1)S(1)}, bf16[256,512]{1,0:T(8,128)(2,1)S(1)}, u32[]{:S(2)}, u32[]{:S(2)}) collective-permute-start(bf16[256,512]{1,0:T(8,128)(2,1)S(1)} %get-tuple-element.59.refs_6_), channel_id=1, source_target_pairs={{0,4},{1,5},{2,6},{3,7},{4,0},{5,1},{6,2},{7,3},{8,12},{9,13},{10,... | collective-permute-start | bytes 786440 | tf_op jit(solution)/shard_map/ppermute | solution.py:45
  38.9 15.0 %collective-permute-start.12 = (bf16[432,512]{1,0:T(8,128)(2,1)S(1)}, bf16[432,512]{1,0:T(8,128)(2,1)S(1)}, u32[]{:S(2)}, u32[]{:S(2)}) collective-permute-start(bf16[432,512]{1,0:T(8,128)(2,1)S(1)} %get-tuple-element.75), channel_id=1, source_target_pairs={{0,1},{1,2},{2,3},{3,0},{4,5},{5,6},{6,7},{7,4},{8,9},{9,10},{10,1... | collective-permute-start | bytes 1327112 | tf_op jit(solution)/shard_map/ppermute | solution.py:41
  41.6 12.3 %collective-permute-start.13 = (bf16[432,512]{1,0:T(8,128)(2,1)S(1)}, bf16[432,512]{1,0:T(8,128)(2,1)S(1)}, u32[]{:S(2)}, u32[]{:S(2)}) collective-permute-start(bf16[432,512]{1,0:T(8,128)(2,1)S(1)} %get-tuple-element.76), channel_id=1, source_target_pairs={{0,3},{1,0},{2,1},{3,2},{4,7},{5,4},{6,5},{7,6},{8,11},{9,8},{10,9... | collective-permute-start | bytes 1327112 | tf_op jit(solution)/shard_map/ppermute | solution.py:41
  41.6 12.3 %collective-permute-start.14 = (bf16[224,512]{1,0:T(8,128)(2,1)S(1)}, bf16[224,512]{1,0:T(8,128)(2,1)S(1)}, u32[]{:S(2)}, u32[]{:S(2)}) collective-permute-start(bf16[224,512]{1,0:T(8,128)(2,1)S(1)} %get-tuple-element.77), channel_id=1, source_target_pairs={{0,4},{1,5},{2,6},{3,7},{4,0},{5,1},{6,2},{7,3},{8,12},{9,13},{10,... | collective-permute-start | bytes 688136 | tf_op jit(solution)/shard_map/ppermute | solution.py:45
  43.3 5.7 %collective-permute-start.17 = (bf16[64,512]{1,0:T(8,128)(2,1)S(1)}, bf16[64,512]{1,0:T(8,128)(2,1)S(1)}, u32[]{:S(2)}, u32[]{:S(2)}) collective-permute-start(bf16[64,512]{1,0:T(8,128)(2,1)S(1)} %get-tuple-element.81.refs_1_), channel_id=1, source_target_pairs={{0,64},{8,72},{16,80},{24,88},{32,96},{40,104},{48,112},{56,120},{... | collective-permute-start | bytes 196616 | tf_op jit(solution)/shard_map/ppermute | solution.py:65
  49.0 23.2 %collective-permute-start.18 = (bf16[672,512]{1,0:T(8,128)(2,1)S(1)}, bf16[672,512]{1,0:T(8,128)(2,1)S(1)}, u32[]{:S(2)}, u32[]{:S(2)}) collective-permute-start(bf16[672,512]{1,0:T(8,128)(2,1)S(1)} %get-tuple-element.82), channel_id=1, source_target_pairs={{0,4},{1,5},{2,6},{3,7},{4,0},{5,1},{6,2},{7,3},{8,12},{9,13},{10,... | collective-permute-start | bytes 2064392 | tf_op jit(solution)/shard_map/ppermute | solution.py:45
  54.1 18.2 %collective-permute-start.15 = (bf16[576,512]{1,0:T(8,128)(2,1)S(1)}, bf16[576,512]{1,0:T(8,128)(2,1)S(1)}, u32[]{:S(2)}, u32[]{:S(2)}) collective-permute-start(bf16[576,512]{1,0:T(8,128)(2,1)S(1)} %get-tuple-element.78), channel_id=1, source_target_pairs={{0,1},{1,2},{2,3},{3,0},{4,5},{5,6},{6,7},{7,4},{8,9},{9,10},{10,1... | collective-permute-start | bytes 1769480 | tf_op jit(solution)/shard_map/ppermute | solution.py:41
  57.4 14.9 %collective-permute-start.16 = (bf16[512,512]{1,0:T(8,128)(2,1)S(1)}, bf16[512,512]{1,0:T(8,128)(2,1)S(1)}, u32[]{:S(2)}, u32[]{:S(2)}) collective-permute-start(bf16[512,512]{1,0:T(8,128)(2,1)S(1)} %get-tuple-element.79.refs_12_), channel_id=1, source_target_pairs={{0,3},{1,0},{2,1},{3,2},{4,7},{5,4},{6,5},{7,6},{8,11},{9,8},{10,9... | collective-permute-start | bytes 1572872 | tf_op jit(solution)/shard_map/ppermute | solution.py:41
  57.4 14.8 %collective-permute-start.19 = (bf16[64,512]{1,0:T(8,128)(2,1)S(1)}, bf16[64,512]{1,0:T(8,128)(2,1)S(1)}, u32[]{:S(2)}, u32[]{:S(2)}) collective-permute-start(bf16[64,512]{1,0:T(8,128)(2,1)S(1)} %get-tuple-element.83.refs_6_), channel_id=1, source_target_pairs={{0,192},{8,200},{16,208},{24,216},{32,224},{40,232},{48,240},{56,2... | collective-permute-start | bytes 196616 | tf_op jit(solution)/shard_map/ppermute | solution.py:65
  72.5 10.6 %collective-permute-start.21 = (bf16[288,512]{1,0:T(8,128)(2,1)S(1)}, bf16[288,512]{1,0:T(8,128)(2,1)S(1)}, u32[]{:S(2)}, u32[]{:S(2)}) collective-permute-start(bf16[288,512]{1,0:T(8,128)(2,1)S(1)} %get-tuple-element.86), channel_id=1, source_target_pairs={{0,4},{1,5},{2,6},{3,7},{4,0},{5,1},{6,2},{7,3},{8,12},{9,13},{10,... | collective-permute-start | bytes 884744 | tf_op jit(solution)/shard_map/ppermute | solution.py:45
  72.6 6.8 %collective-permute-start.22 = (bf16[224,512]{1,0:T(8,128)(2,1)S(1)}, bf16[224,512]{1,0:T(8,128)(2,1)S(1)}, u32[]{:S(2)}, u32[]{:S(2)}) collective-permute-start(bf16[224,512]{1,0:T(8,128)(2,1)S(1)} %get-tuple-element.87), channel_id=1, source_target_pairs={{0,1},{1,2},{2,3},{3,0},{4,5},{5,6},{6,7},{7,4},{8,9},{9,10},{10,1... | collective-permute-start | bytes 688136 | tf_op jit(solution)/shard_map/ppermute | solution.py:41
  75.9 7.2 %collective-permute-start.23 = (bf16[224,512]{1,0:T(8,128)(2,1)S(1)}, bf16[224,512]{1,0:T(8,128)(2,1)S(1)}, u32[]{:S(2)}, u32[]{:S(2)}) collective-permute-start(bf16[224,512]{1,0:T(8,128)(2,1)S(1)} %get-tuple-element.88), channel_id=1, source_target_pairs={{0,3},{1,0},{2,1},{3,2},{4,7},{5,4},{6,5},{7,6},{8,11},{9,8},{10,9... | collective-permute-start | bytes 688136 | tf_op jit(solution)/shard_map/ppermute | solution.py:41
  75.9 1.3 %collective-permute-start.20 = (bf16[64,512]{1,0:T(8,128)(2,1)S(1)}, bf16[64,512]{1,0:T(8,128)(2,1)S(1)}, u32[]{:S(2)}, u32[]{:S(2)}) collective-permute-start(bf16[64,512]{1,0:T(8,128)(2,1)S(1)} %get-tuple-element.84.refs_5_), channel_id=1, source_target_pairs={{0,8},{8,0},{16,24},{24,16},{32,40},{40,32},{48,56},{56,48},{64,72... | collective-permute-start | bytes 196616 | tf_op jit(solution)/shard_map/ppermute | solution.py:49
  (2 other events, 20.9 us)

commit v3 on v2

--- a/solution.py
+++ b/solution.py
@@ -193,15 +193,18 @@
     share[...] = add_rounded(mine[...], other[...])
 
 
-def second_kernel(w_lo, w_hi, back_hi, next_hi, z_lo, mine, other, to_next, to_back, to_z, share):
+def second_y_kernel(w_lo, back_hi, z_lo, mine, other, to_next, to_back, share):
     to_next[:HALF] = z_lo[...]
     to_next[HALF:] = back_hi[...]
     to_back[:HALF] = z_lo[...]
     to_back[HALF:] = w_lo[...]
+    share[...] = add_rounded(mine[...], other[...])
+
+
+def second_z_kernel(w_hi, back_hi, next_hi, to_z):
     to_z[:HALF] = w_hi[...]
     to_z[HALF : 2 * HALF] = next_hi[...]
     to_z[2 * HALF :] = back_hi[...]
-    share[...] = add_rounded(mine[...], other[...])
 
 
 def third_kernel(w_lo, y_back, y_next, mine, other, to_next, to_back, to_z, share):
@@ -303,12 +306,13 @@
     )[0]
 
 
-def join_second_kernel(
-    p11_lo, p13_lo, p01, p02_hi, from_back, from_next, in02_hi, to_next, to_back
-):
+def join_second_a_kernel(p11_lo, p01, from_back, to_next):
     to_next[:SOME] = add_rounded(p11_lo[:SOME], from_back[:SOME])
     to_next[SOME:LOWER] = p11_lo[SOME:]
     to_next[LOWER:] = add_rounded(p01[:LOWER], from_back[SOME:])
+
+
+def join_second_b_kernel(p13_lo, p02_hi, from_next, in02_hi, to_back):
     to_back[:SOME] = p13_lo[:SOME]
     to_back[SOME:LOWER] = add_rounded(p13_lo[SOME:], from_next[:SOME])
     to_back[LOWER:] = add_rounded(p02_hi[...], in02_hi[...])
@@ -410,13 +414,16 @@
     mine, theirs = leaving(where, plan, weights, outer_params, [(w, False)])
     other = swap_core(theirs)
 
-    to_next, to_back, to_z, share = local_call(
-        second_kernel,
-        [rows16(2 * HALF), rows16(2 * HALF), rows16(3 * HALF), share_rows],
-        [],
-        [],
-        near=[w_lo, w_hi, back_hi, next_hi, z_lo, mine, other],
-    )
+    to_next, to_back, share = local_call(
+        second_y_kernel,
+        [rows16(2 * HALF), rows16(2 * HALF), share_rows],
+        [],
+        [],
+        near=[w_lo, back_hi, z_lo, mine, other],
+    )
+    to_z = local_call(
+        second_z_kernel, [rows16(3 * HALF)], [], [], near=[w_hi, back_hi, next_hi]
+    )[0]
     z_hi, y_back, y_next = move_z(to_z), move_y(to_next, 1), move_y(to_back, -1)
     slabs, turned, goal = turn(where, activations, target, [(share, False)])
     share = add_share(share, swap_x(share, 1))
@@ -481,13 +488,17 @@
     )
     in_hi = move_z(to_z)
 
-    to_next, to_back = local_call(
-        join_second_kernel,
-        [rows16(2 * LOWER), rows16(SLAB)],
-        [],
-        [],
-        near=[p11_lo, p13_lo, p01, p02_hi, from_back, from_next, in02_hi],
-    )
+    to_next = local_call(
+        join_second_a_kernel, [rows16(2 * LOWER)], [], [], near=[p11_lo, p01, from_back]
+    )[0]
+    to_back = local_call(
+        join_second_b_kernel,
+        [rows16(SLAB)],
+        [],
+        [],
+        near=[p13_lo, p02_hi, from_next, in02_hi],
+        late=[(to_next, False)],
+    )[0]
     from_back, from_next = move_y(to_next, 1), move_y(to_back, -1)
     low2 = from_back
     other = swap_z(share, 3)

time: 85.5 us -> 83.7 us (0.979)
  starting transfers between devices: 39.7 us -> 37.3 us
    ppermute x6, starting transfers between devices: 12.6 us -> 5.58 us  [move_z(): return lax.ppermute(value, 'fsdp', [(i, (i + 4) % 8) for i in range(8)])]
    ppermute x12, starting transfers between devices: 16.8 us -> 19.7 us  [move_y(): return lax.ppermute(value, 'fsdp', pairs)]
    ppermute x2, starting transfers between devices: 5.93 us -> 7.63 us  [swap_z(): return lax.ppermute(value, 'rep', pairs)]
    pallas_call x15 -> x17, Pallas kernels: 21.1 us -> 21.1 us  [local_call(): pl.pallas_call(run, out_shape=outs, in_specs=[SMEM] * len(scalars) + [VME...]
  transfers between devices with their start and end apart: 24 -> 24, of which waited for: 11 -> 14; matrix products, arithmetic and copies ran while one was open for 0% -> 0% of each run, Pallas kernels for 19% -> 19%
where the time goes in v3:
time: 83.7 us; the launch traced here: 83.5 us
  starting transfers between devices  37.3 us (45%)
  waiting for transfers between devices  23.4 us (28%)
  Pallas kernels  21.1 us (25%)
  between operations  0.96 us (1%)
    pallas_call x17, Pallas kernels, local_call(): pl.pallas_call(run, out_shape=outs, in_specs=[SMEM] * len(scalars) + [VME...  21.1 us
    ppermute x12, starting transfers between devices, move_y(): return lax.ppermute(value, 'fsdp', pairs)  19.7 us
    ppermute x2, waiting for transfers between devices, swap_z(): return lax.ppermute(value, 'rep', pairs)  8.74 us
    ppermute x12, waiting for transfers between devices, move_y(): return lax.ppermute(value, 'fsdp', pairs)  8.42 us
    ppermute x2, starting transfers between devices, swap_z(): return lax.ppermute(value, 'rep', pairs)  7.63 us
    ppermute x6, starting transfers between devices, move_z(): return lax.ppermute(value, 'fsdp', [(i, (i + 4) % 8) for i in range(8)])  5.58 us
    ppermute x2, starting transfers between devices, swap_x(): return lax.ppermute(value, 'rep', pairs)  4.34 us
    ppermute x2, waiting for transfers between devices, swap_x(): return lax.ppermute(value, 'rep', pairs)  2.78 us
  transfers between devices with their start and end apart: 24, of which 14 were waited for; matrix products, arithmetic and copies ran while one was open for 0% of the time, Pallas kernels for 19%

profile of v3, /device:TPU:24, one launch (start us, length us, event | category | flops | bytes accessed | tf_op | source)
XLA Modules:
  0.0 83.5 jit_solution(13408586343024063562)
XLA Ops:
  1.9 2.0 %collective-permute-start = (bf16[256,512]{1,0:T(8,128)(2,1)S(1)}, bf16[256,512]{1,0:T(8,128)(2,1)S(1)}, u32[]{:S(2)}, u32[]{:S(2)}) collective-permute-start(bf16[256,512]{1,0:T(8,128)(2,1)S(1)} %get-tuple-element.48.refs_0_), channel_id=1, source_target_pairs={{0,1},{1,2},{2,3},{3,0},{4,5},{5,6},{6,7},{7,4},{8,9},{9,10},{10,1... | collective-permute-start | bytes 786440 | tf_op jit(solution)/shard_map/ppermute | solution.py:41
  4.1 1.8 %collective-permute-start.7 = (bf16[256,512]{1,0:T(8,128)(2,1)S(1)}, bf16[256,512]{1,0:T(8,128)(2,1)S(1)}, u32[]{:S(2)}, u32[]{:S(2)}) collective-permute-start(bf16[256,512]{1,0:T(8,128)(2,1)S(1)} %get-tuple-element.48.refs_0_), channel_id=1, source_target_pairs={{0,3},{1,0},{2,1},{3,2},{4,7},{5,4},{6,5},{7,6},{8,11},{9,8},{10,9... | collective-permute-start | bytes 786440 | tf_op jit(solution)/shard_map/ppermute | solution.py:41
  6.6 1.6 %shard_map.128 = (bf16[64,512]{1,0:T(8,128)(2,1)S(1)}, bf16[64,512]{1,0:T(8,128)(2,1)S(1)}) custom-call(s32[2]{0:T(128)S(1)} %pad_add_fusion.refs_0_, s32[4]{0:T(128)S(1)} %copy-done, f32[512,512]{1,0:T(8,128)} %bitcast.7, f32[512,512]{1,0:T(8,128)} %refs_1_.6, bf16[512,512]{1,0:T(8,128)(2,1)S(1)} %get-tuple-element.49.refs_4_.refs_1_.refs_2_), custom_call_target="tpu_custom_call" | custom-call | flops 1024 | bytes 1024 | tf_op jit(solution)/shard_map/pallas_call | solution.py:109
  10.4 1.5 %collective-permute-start.3 = (bf16[512,512]{1,0:T(8,128)(2,1)S(1)}, bf16[512,512]{1,0:T(8,128)(2,1)S(1)}, u32[]{:S(2)}, u32[]{:S(2)}) collective-permute-start(bf16[512,512]{1,0:T(8,128)(2,1)S(1)} %get-tuple-element.52), channel_id=1, source_target_pairs={{0,1},{1,2},{2,3},{3,0},{4,5},{5,6},{6,7},{7,4},{8,9},{9,10},{10,1... | collective-permute-start | bytes 1572872 | tf_op jit(solution)/shard_map/ppermute | solution.py:41
  14.4 1.5 %collective-permute-start.5 = (bf16[64,512]{1,0:T(8,128)(2,1)S(1)}, bf16[64,512]{1,0:T(8,128)(2,1)S(1)}, u32[]{:S(2)}, u32[]{:S(2)}) collective-permute-start(bf16[64,512]{1,0:T(8,128)(2,1)S(1)} %get-tuple-element.54.refs_0_.refs_3_), channel_id=1, source_target_pairs={{0,16},{8,24},{16,0},{24,8},{32,48},{40,56},{48,32},{56,40},{64,80... | collective-permute-start | bytes 196616 | tf_op jit(solution)/shard_map/ppermute | solution.py:57
  15.8 2.8 %collective-permute-done.5.refs_1_ = bf16[64,512]{1,0:T(8,128)(2,1)S(1)} collective-permute-done((bf16[64,512]{1,0:T(8,128)(2,1)S(1)}, bf16[64,512]{1,0:T(8,128)(2,1)S(1)}, u32[]{:S(2)}, u32[]{:S(2)}) %collective-permute-start.5) | collective-permute-done | bytes 65568 | tf_op jit(solution)/shard_map/ppermute | solution.py:57
  18.6 2.8 %collective-permute-start.6 = (bf16[64,512]{1,0:T(8,128)(2,1)S(1)}, bf16[64,512]{1,0:T(8,128)(2,1)S(1)}, u32[]{:S(2)}, u32[]{:S(2)}) collective-permute-start(bf16[64,512]{1,0:T(8,128)(2,1)S(1)} %shard_map.130.refs_3_), channel_id=1, source_target_pairs={{0,48},{8,56},{16,32},{24,40},{32,16},{40,24},{48,0},{56,8},{64,11... | collective-permute-start | bytes 196616 | tf_op jit(solution)/shard_map/ppermute | solution.py:57
  21.5 3.2 %shard_map.131 = (bf16[8,512,512]{2,1,0:T(8,128)(2,1)S(1)}, bf16[8,512,512]{2,1,0:T(8,128)(2,1)S(1)}, bf16[512,512]{1,0:T(8,128)(2,1)S(1)}) custom-call(s32[2]{0:T(128)S(1)} %pad_add_fusion.refs_0_, bf16[512,4096]{1,0:T(8,128)(2,1)} %refs_1_.5, bf16[512,512]{1,0:T(8,128)(2,1)} %refs_2_.2, bf16[64,512]{1,0:T(8,128)(2,1)S(1)} %get-tuple-element.54.refs_0_.refs_3_), custom_call_target="tpu_custom_call" | custom-call | flops 1024 | bytes 1024 | tf_op jit(solution)/shard_map/pallas_call | solution.py:109
  26.6 3.0 %collective-permute-start.9 = (bf16[384,512]{1,0:T(8,128)(2,1)S(1)}, bf16[384,512]{1,0:T(8,128)(2,1)S(1)}, u32[]{:S(2)}, u32[]{:S(2)}) collective-permute-start(bf16[384,512]{1,0:T(8,128)(2,1)S(1)} %get-tuple-element.62), channel_id=1, source_target_pairs={{0,1},{1,2},{2,3},{3,0},{4,5},{5,6},{6,7},{7,4},{8,9},{9,10},{10,1... | collective-permute-start | bytes 1179656 | tf_op jit(solution)/shard_map/ppermute | solution.py:41
  29.5 1.8 %collective-permute-start.11 = (bf16[256,512]{1,0:T(8,128)(2,1)S(1)}, bf16[256,512]{1,0:T(8,128)(2,1)S(1)}, u32[]{:S(2)}, u32[]{:S(2)}) collective-permute-start(bf16[256,512]{1,0:T(8,128)(2,1)S(1)} %get-tuple-element.56.refs_6_), channel_id=1, source_target_pairs={{0,4},{1,5},{2,6},{3,7},{4,0},{5,1},{6,2},{7,3},{8,12},{9,13},{10,... | collective-permute-start | bytes 786440 | tf_op jit(solution)/shard_map/ppermute | solution.py:45
  31.4 3.6 %shard_map.133 = (f32[128,512]{1,0:T(8,128)S(1)}, f32[512,512]{1,0:T(8,128)S(1)}, f32[512,512]{1,0:T(8,128)S(1)}, f32[512,512]{1,0:T(8,128)}, f32[512,512]{1,0:T(8,128)}) custom-call(s32[4]{0:T(128)S(1)} %copy-done.1, f32[512,512]{1,0:T(8,128)} %refs_1_.6, f32[512,512]{1,0:T(8,128)} %refs_2_.3, f32[128,512]{1,0:T(8,128)} %refs_3_.3, f32[512,512]{1,0:T(8,128)} %bitcast.8, ...), custom_call_target="tpu_custom_call" | custom-call | flops 1024 | bytes 1024 | tf_op jit(solution)/shard_map/pallas_call | solution.py:109
  35.0 1.8 %shard_map.135.refs_2_ = f32[512,512]{1,0:T(8,128)S(1)} custom-call(bf16[8,512,512]{2,1,0:T(8,128)(2,1)S(1)} %get-tuple-element.61.refs_0_, bf16[512,512]{1,0:T(8,128)(2,1)S(1)} %get-tuple-element.49.refs_4_.refs_1_.refs_2_, bf16[256,512]{1,0:T(8,128)(2,1)S(1)} %collective-permute-done.7.refs_2_.refs_3_, ...), custom_call_target="tpu_custom_call" | custom-call | flops 1024 | bytes 1024 | tf_op jit(solution)/shard_map/pallas_call | solution.py:109
  36.9 1.6 %shard_map.136 = (bf16[512,512]{1,0:T(8,128)(2,1)S(1)}, bf16[432,512]{1,0:T(8,128)(2,1)S(1)}, bf16[432,512]{1,0:T(8,128)(2,1)S(1)}, bf16[224,512]{1,0:T(8,128)(2...) custom-call(bf16[8,512,512]{2,1,0:T(8,128)(2,1)S(1)} %get-tuple-element.61.refs_0_, ...), custom_call_target="tpu_custom_call" | custom-call | flops 1024 | bytes 1024 | tf_op jit(solution)/shard_map/pallas_call | solution.py:109
  38.5 3.2 %collective-permute-start.12 = (bf16[432,512]{1,0:T(8,128)(2,1)S(1)}, bf16[432,512]{1,0:T(8,128)(2,1)S(1)}, u32[]{:S(2)}, u32[]{:S(2)}) collective-permute-start(bf16[432,512]{1,0:T(8,128)(2,1)S(1)} %get-tuple-element.69), channel_id=1, source_target_pairs={{0,1},{1,2},{2,3},{3,0},{4,5},{5,6},{6,7},{7,4},{8,9},{9,10},{10,1... | collective-permute-start | bytes 1327112 | tf_op jit(solution)/shard_map/ppermute | solution.py:41
  41.7 3.3 %collective-permute-start.17 = (bf16[64,512]{1,0:T(8,128)(2,1)S(1)}, bf16[64,512]{1,0:T(8,128)(2,1)S(1)}, u32[]{:S(2)}, u32[]{:S(2)}) collective-permute-start(bf16[64,512]{1,0:T(8,128)(2,1)S(1)} %get-tuple-element.75.refs_1_), channel_id=1, source_target_pairs={{0,64},{8,72},{16,80},{24,88},{32,96},{40,104},{48,112},{56,120},{... | collective-permute-start | bytes 196616 | tf_op jit(solution)/shard_map/ppermute | solution.py:65
  45.7 1.5 %shard_map.137 = (bf16[288,512]{1,0:T(8,128)(2,1)S(1)}, bf16[288,512]{1,0:T(8,128)(2,1)S(1)}, bf16[288,512]{1,0:T(8,128)(2,1)S(1)}, bf16[672,512]{1,0:T(8,128)(2...) custom-call(bf16[8,512,512]{2,1,0:T(8,128)(2,1)S(1)} %get-tuple-element.60.refs_1_.refs_0_, ...), custom_call_target="tpu_custom_call" | custom-call | flops 1024 | bytes 1024 | tf_op jit(solution)/shard_map/pallas_call | solution.py:109
  49.1 3.8 %collective-permute-start.13 = (bf16[576,512]{1,0:T(8,128)(2,1)S(1)}, bf16[576,512]{1,0:T(8,128)(2,1)S(1)}, u32[]{:S(2)}, u32[]{:S(2)}) collective-permute-start(bf16[576,512]{1,0:T(8,128)(2,1)S(1)} %shard_map.138.refs_4_), channel_id=1, source_target_pairs={{0,1},{1,2},{2,3},{3,0},{4,5},{5,6},{6,7},{7,4},{8,9},{9,10},{10,1... | collective-permute-start | bytes 1769480 | tf_op jit(solution)/shard_map/ppermute | solution.py:41
  53.7 4.4 %collective-permute-start.19 = (bf16[64,512]{1,0:T(8,128)(2,1)S(1)}, bf16[64,512]{1,0:T(8,128)(2,1)S(1)}, u32[]{:S(2)}, u32[]{:S(2)}) collective-permute-start(bf16[64,512]{1,0:T(8,128)(2,1)S(1)} %get-tuple-element.77.refs_6_), channel_id=1, source_target_pairs={{0,192},{8,200},{16,208},{24,216},{32,224},{40,232},{48,240},{56,2... | collective-permute-start | bytes 196616 | tf_op jit(solution)/shard_map/ppermute | solution.py:65
  58.1 3.8 %shard_map.141.refs_8_ = bf16[512,4096]{1,0:T(8,128)(2,1)} custom-call(s32[2]{0:T(128)S(1)} %pad_add_fusion.refs_0_, bf16[512,512]{1,0:T(8,128)(2,1)S(1)} %get-tuple-element.64.refs_1_, bf16[512,512]{1,0:T(8,128)(2,1)S(1)} %get-tuple-element.49.refs_4_.refs_1_.refs_2_, bf16[256,512]{1,0:T(8,128)(2,1)S(1)} %collective-permute-done.7.refs_2_.refs_3_, ...), custom_call_target="tpu_custom_call" | custom-call | flops 1024 | bytes 1024 | tf_op jit(solution)/shard_map/pallas_call | solution.py:109
  61.9 8.5 %collective-permute-done.19.refs_7_ = bf16[64,512]{1,0:T(8,128)(2,1)S(1)} collective-permute-done((bf16[64,512]{1,0:T(8,128)(2,1)S(1)}, bf16[64,512]{1,0:T(8,128)(2,1)S(1)}, u32[]{:S(2)}, u32[]{:S(2)}) %collective-permute-start.19) | collective-permute-done | bytes 65568 | tf_op jit(solution)/shard_map/ppermute | solution.py:65
  70.7 3.3 %collective-permute-start.22 = (bf16[224,512]{1,0:T(8,128)(2,1)S(1)}, bf16[224,512]{1,0:T(8,128)(2,1)S(1)}, u32[]{:S(2)}, u32[]{:S(2)}) collective-permute-start(bf16[224,512]{1,0:T(8,128)(2,1)S(1)} %get-tuple-element.81), channel_id=1, source_target_pairs={{0,1},{1,2},{2,3},{3,0},{4,5},{5,6},{6,7},{7,4},{8,9},{9,10},{10,1... | collective-permute-start | bytes 688136 | tf_op jit(solution)/shard_map/ppermute | solution.py:41
  75.3 2.3 %collective-permute-done.22.refs_12_ = bf16[224,512]{1,0:T(8,128)(2,1)S(1)} collective-permute-done((bf16[224,512]{1,0:T(8,128)(2,1)S(1)}, bf16[224,512]{1,0:T(8,128)(2,1)S(1)}, u32[]{:S(2)}, u32[]{:S(2)}) %collective-permute-start.22) | collective-permute-done | bytes 229408 | tf_op jit(solution)/shard_map/ppermute | solution.py:41
  77.6 3.7 %collective-permute-done.23.refs_13_ = bf16[224,512]{1,0:T(8,128)(2,1)S(1)} collective-permute-done((bf16[224,512]{1,0:T(8,128)(2,1)S(1)}, bf16[224,512]{1,0:T(8,128)(2,1)S(1)}, u32[]{:S(2)}, u32[]{:S(2)}) %collective-permute-start.23) | collective-permute-done | bytes 229408 | tf_op jit(solution)/shard_map/ppermute | solution.py:41
  81.3 2.0 %shard_map.143 = (f32[512,512]{1,0:T(8,128)}, f32[512,512]{1,0:T(8,128)}, f32[128,512]{1,0:T(8,128)}) custom-call(s32[2]{0:T(128)S(1)} %pad_add_fusion.refs_0_, s32[4]{0:T(128)S(1)} %copy-done.1, f32[128,512]{1,0:T(8,128)S(1)} %get-tuple-element.57.refs_8_.refs_2_, f32[512,512]{1,0:T(8,128)S(1)} %get-tuple-element.58.refs_3_, ...), custom_call_target="tpu_custom_call" | custom-call | flops 1024 | bytes 1024 | tf_op jit(solution)/shard_map/pallas_call | solution.py:109
  (46 shorter events, 13.7 us)
Async XLA Ops:
  1.9 8.1 %collective-permute-start = (bf16[256,512]{1,0:T(8,128)(2,1)S(1)}, bf16[256,512]{1,0:T(8,128)(2,1)S(1)}, u32[]{:S(2)}, u32[]{:S(2)}) collective-permute-start(bf16[256,512]{1,0:T(8,128)(2,1)S(1)} %get-tuple-element.48.refs_0_), channel_id=1, source_target_pairs={{0,1},{1,2},{2,3},{3,0},{4,5},{5,6},{6,7},{7,4},{8,9},{9,10},{10,1... | collective-permute-start | bytes 786440 | tf_op jit(solution)/shard_map/ppermute | solution.py:41
  3.9 6.4 %collective-permute-start.1 = (bf16[256,512]{1,0:T(8,128)(2,1)S(1)}, bf16[256,512]{1,0:T(8,128)(2,1)S(1)}, u32[]{:S(2)}, u32[]{:S(2)}) collective-permute-start(bf16[256,512]{1,0:T(8,128)(2,1)S(1)} %get-tuple-element.47.refs_0_), channel_id=1, source_target_pairs={{0,4},{1,5},{2,6},{3,7},{4,0},{5,1},{6,2},{7,3},{8,12},{9,13},{10,... | collective-permute-start | bytes 786440 | tf_op jit(solution)/shard_map/ppermute | solution.py:45
  4.1 8.9 %collective-permute-start.7 = (bf16[256,512]{1,0:T(8,128)(2,1)S(1)}, bf16[256,512]{1,0:T(8,128)(2,1)S(1)}, u32[]{:S(2)}, u32[]{:S(2)}) collective-permute-start(bf16[256,512]{1,0:T(8,128)(2,1)S(1)} %get-tuple-element.48.refs_0_), channel_id=1, source_target_pairs={{0,3},{1,0},{2,1},{3,2},{4,7},{5,4},{6,5},{7,6},{8,11},{9,8},{10,9... | collective-permute-start | bytes 786440 | tf_op jit(solution)/shard_map/ppermute | solution.py:41
  8.3 1.3 %collective-permute-start.2 = (bf16[64,512]{1,0:T(8,128)(2,1)S(1)}, bf16[64,512]{1,0:T(8,128)(2,1)S(1)}, u32[]{:S(2)}, u32[]{:S(2)}) collective-permute-start(bf16[64,512]{1,0:T(8,128)(2,1)S(1)} %get-tuple-element.51), channel_id=1, source_target_pairs={{0,8},{8,0},{16,24},{24,16},{32,40},{40,32},{48,56},{56,48},{64,72... | collective-permute-start | bytes 196616 | tf_op jit(solution)/shard_map/ppermute | solution.py:49
  10.4 14.3 %collective-permute-start.3 = (bf16[512,512]{1,0:T(8,128)(2,1)S(1)}, bf16[512,512]{1,0:T(8,128)(2,1)S(1)}, u32[]{:S(2)}, u32[]{:S(2)}) collective-permute-start(bf16[512,512]{1,0:T(8,128)(2,1)S(1)} %get-tuple-element.52), channel_id=1, source_target_pairs={{0,1},{1,2},{2,3},{3,0},{4,5},{5,6},{6,7},{7,4},{8,9},{9,10},{10,1... | collective-permute-start | bytes 1572872 | tf_op jit(solution)/shard_map/ppermute | solution.py:41
  11.9 14.3 %collective-permute-start.4 = (bf16[512,512]{1,0:T(8,128)(2,1)S(1)}, bf16[512,512]{1,0:T(8,128)(2,1)S(1)}, u32[]{:S(2)}, u32[]{:S(2)}) collective-permute-start(bf16[512,512]{1,0:T(8,128)(2,1)S(1)} %get-tuple-element.53), channel_id=1, source_target_pairs={{0,3},{1,0},{2,1},{3,2},{4,7},{5,4},{6,5},{7,6},{8,11},{9,8},{10,9... | collective-permute-start | bytes 1572872 | tf_op jit(solution)/shard_map/ppermute | solution.py:41
  13.0 22.0 %collective-permute-start.8 = (bf16[768,512]{1,0:T(8,128)(2,1)S(1)}, bf16[768,512]{1,0:T(8,128)(2,1)S(1)}, u32[]{:S(2)}, u32[]{:S(2)}) collective-permute-start(bf16[768,512]{1,0:T(8,128)(2,1)S(1)} %shard_map.134), channel_id=1, source_target_pairs={{0,4},{1,5},{2,6},{3,7},{4,0},{5,1},{6,2},{7,3},{8,12},{9,13},{10,... | collective-permute-start | bytes 2359304 | tf_op jit(solution)/shard_map/ppermute | solution.py:45
  14.4 4.3 %collective-permute-start.5 = (bf16[64,512]{1,0:T(8,128)(2,1)S(1)}, bf16[64,512]{1,0:T(8,128)(2,1)S(1)}, u32[]{:S(2)}, u32[]{:S(2)}) collective-permute-start(bf16[64,512]{1,0:T(8,128)(2,1)S(1)} %get-tuple-element.54.refs_0_.refs_3_), channel_id=1, source_target_pairs={{0,16},{8,24},{16,0},{24,8},{32,48},{40,56},{48,32},{56,40},{64,80... | collective-permute-start | bytes 196616 | tf_op jit(solution)/shard_map/ppermute | solution.py:57
  18.6 6.1 %collective-permute-start.6 = (bf16[64,512]{1,0:T(8,128)(2,1)S(1)}, bf16[64,512]{1,0:T(8,128)(2,1)S(1)}, u32[]{:S(2)}, u32[]{:S(2)}) collective-permute-start(bf16[64,512]{1,0:T(8,128)(2,1)S(1)} %shard_map.130.refs_3_), channel_id=1, source_target_pairs={{0,48},{8,56},{16,32},{24,40},{32,16},{40,24},{48,0},{56,8},{64,11... | collective-permute-start | bytes 196616 | tf_op jit(solution)/shard_map/ppermute | solution.py:57
  26.2 10.6 %collective-permute-start.10 = (bf16[384,512]{1,0:T(8,128)(2,1)S(1)}, bf16[384,512]{1,0:T(8,128)(2,1)S(1)}, u32[]{:S(2)}, u32[]{:S(2)}) collective-permute-start(bf16[384,512]{1,0:T(8,128)(2,1)S(1)} %get-tuple-element.63), channel_id=1, source_target_pairs={{0,3},{1,0},{2,1},{3,2},{4,7},{5,4},{6,5},{7,6},{8,11},{9,8},{10,9... | collective-permute-start | bytes 1179656 | tf_op jit(solution)/shard_map/ppermute | solution.py:41
  26.6 10.3 %collective-permute-start.9 = (bf16[384,512]{1,0:T(8,128)(2,1)S(1)}, bf16[384,512]{1,0:T(8,128)(2,1)S(1)}, u32[]{:S(2)}, u32[]{:S(2)}) collective-permute-start(bf16[384,512]{1,0:T(8,128)(2,1)S(1)} %get-tuple-element.62), channel_id=1, source_target_pairs={{0,1},{1,2},{2,3},{3,0},{4,5},{5,6},{6,7},{7,4},{8,9},{9,10},{10,1... | collective-permute-start | bytes 1179656 | tf_op jit(solution)/shard_map/ppermute | solution.py:41
  29.5 7.2 %collective-permute-start.11 = (bf16[256,512]{1,0:T(8,128)(2,1)S(1)}, bf16[256,512]{1,0:T(8,128)(2,1)S(1)}, u32[]{:S(2)}, u32[]{:S(2)}) collective-permute-start(bf16[256,512]{1,0:T(8,128)(2,1)S(1)} %get-tuple-element.56.refs_6_), channel_id=1, source_target_pairs={{0,4},{1,5},{2,6},{3,7},{4,0},{5,1},{6,2},{7,3},{8,12},{9,13},{10,... | collective-permute-start | bytes 786440 | tf_op jit(solution)/shard_map/ppermute | solution.py:45
  38.5 10.5 %collective-permute-start.12 = (bf16[432,512]{1,0:T(8,128)(2,1)S(1)}, bf16[432,512]{1,0:T(8,128)(2,1)S(1)}, u32[]{:S(2)}, u32[]{:S(2)}) collective-permute-start(bf16[432,512]{1,0:T(8,128)(2,1)S(1)} %get-tuple-element.69), channel_id=1, source_target_pairs={{0,1},{1,2},{2,3},{3,0},{4,5},{5,6},{6,7},{7,4},{8,9},{9,10},{10,1... | collective-permute-start | bytes 1327112 | tf_op jit(solution)/shard_map/ppermute | solution.py:41
  41.7 11.8 %collective-permute-start.14 = (bf16[432,512]{1,0:T(8,128)(2,1)S(1)}, bf16[432,512]{1,0:T(8,128)(2,1)S(1)}, u32[]{:S(2)}, u32[]{:S(2)}) collective-permute-start(bf16[432,512]{1,0:T(8,128)(2,1)S(1)} %get-tuple-element.72), channel_id=1, source_target_pairs={{0,3},{1,0},{2,1},{3,2},{4,7},{5,4},{6,5},{7,6},{8,11},{9,8},{10,9... | collective-permute-start | bytes 1327112 | tf_op jit(solution)/shard_map/ppermute | solution.py:41
  41.7 5.8 %collective-permute-start.17 = (bf16[64,512]{1,0:T(8,128)(2,1)S(1)}, bf16[64,512]{1,0:T(8,128)(2,1)S(1)}, u32[]{:S(2)}, u32[]{:S(2)}) collective-permute-start(bf16[64,512]{1,0:T(8,128)(2,1)S(1)} %get-tuple-element.75.refs_1_), channel_id=1, source_target_pairs={{0,64},{8,72},{16,80},{24,88},{32,96},{40,104},{48,112},{56,120},{... | collective-permute-start | bytes 196616 | tf_op jit(solution)/shard_map/ppermute | solution.py:65
  45.0 8.5 %collective-permute-start.15 = (bf16[224,512]{1,0:T(8,128)(2,1)S(1)}, bf16[224,512]{1,0:T(8,128)(2,1)S(1)}, u32[]{:S(2)}, u32[]{:S(2)}) collective-permute-start(bf16[224,512]{1,0:T(8,128)(2,1)S(1)} %get-tuple-element.73), channel_id=1, source_target_pairs={{0,4},{1,5},{2,6},{3,7},{4,0},{5,1},{6,2},{7,3},{8,12},{9,13},{10,... | collective-permute-start | bytes 688136 | tf_op jit(solution)/shard_map/ppermute | solution.py:45
  47.6 22.8 %collective-permute-start.18 = (bf16[672,512]{1,0:T(8,128)(2,1)S(1)}, bf16[672,512]{1,0:T(8,128)(2,1)S(1)}, u32[]{:S(2)}, u32[]{:S(2)}) collective-permute-start(bf16[672,512]{1,0:T(8,128)(2,1)S(1)} %get-tuple-element.76), channel_id=1, source_target_pairs={{0,4},{1,5},{2,6},{3,7},{4,0},{5,1},{6,2},{7,3},{8,12},{9,13},{10,... | collective-permute-start | bytes 2064392 | tf_op jit(solution)/shard_map/ppermute | solution.py:45
  49.1 21.2 %collective-permute-start.13 = (bf16[576,512]{1,0:T(8,128)(2,1)S(1)}, bf16[576,512]{1,0:T(8,128)(2,1)S(1)}, u32[]{:S(2)}, u32[]{:S(2)}) collective-permute-start(bf16[576,512]{1,0:T(8,128)(2,1)S(1)} %shard_map.138.refs_4_), channel_id=1, source_target_pairs={{0,1},{1,2},{2,3},{3,0},{4,5},{5,6},{6,7},{7,4},{8,9},{9,10},{10,1... | collective-permute-start | bytes 1769480 | tf_op jit(solution)/shard_map/ppermute | solution.py:41
  53.6 16.7 %collective-permute-start.16 = (bf16[512,512]{1,0:T(8,128)(2,1)S(1)}, bf16[512,512]{1,0:T(8,128)(2,1)S(1)}, u32[]{:S(2)}, u32[]{:S(2)}) collective-permute-start(bf16[512,512]{1,0:T(8,128)(2,1)S(1)} %shard_map.139.refs_12_), channel_id=1, source_target_pairs={{0,3},{1,0},{2,1},{3,2},{4,7},{5,4},{6,5},{7,6},{8,11},{9,8},{10,9... | collective-permute-start | bytes 1572872 | tf_op jit(solution)/shard_map/ppermute | solution.py:41
  53.7 16.6 %collective-permute-start.19 = (bf16[64,512]{1,0:T(8,128)(2,1)S(1)}, bf16[64,512]{1,0:T(8,128)(2,1)S(1)}, u32[]{:S(2)}, u32[]{:S(2)}) collective-permute-start(bf16[64,512]{1,0:T(8,128)(2,1)S(1)} %get-tuple-element.77.refs_6_), channel_id=1, source_target_pairs={{0,192},{8,200},{16,208},{24,216},{32,224},{40,232},{48,240},{56,2... | collective-permute-start | bytes 196616 | tf_op jit(solution)/shard_map/ppermute | solution.py:65
  70.6 10.7 %collective-permute-start.21 = (bf16[288,512]{1,0:T(8,128)(2,1)S(1)}, bf16[288,512]{1,0:T(8,128)(2,1)S(1)}, u32[]{:S(2)}, u32[]{:S(2)}) collective-permute-start(bf16[288,512]{1,0:T(8,128)(2,1)S(1)} %get-tuple-element.80), channel_id=1, source_target_pairs={{0,4},{1,5},{2,6},{3,7},{4,0},{5,1},{6,2},{7,3},{8,12},{9,13},{10,... | collective-permute-start | bytes 884744 | tf_op jit(solution)/shard_map/ppermute | solution.py:45
  70.7 6.9 %collective-permute-start.22 = (bf16[224,512]{1,0:T(8,128)(2,1)S(1)}, bf16[224,512]{1,0:T(8,128)(2,1)S(1)}, u32[]{:S(2)}, u32[]{:S(2)}) collective-permute-start(bf16[224,512]{1,0:T(8,128)(2,1)S(1)} %get-tuple-element.81), channel_id=1, source_target_pairs={{0,1},{1,2},{2,3},{3,0},{4,5},{5,6},{6,7},{7,4},{8,9},{9,10},{10,1... | collective-permute-start | bytes 688136 | tf_op jit(solution)/shard_map/ppermute | solution.py:41
  74.1 7.2 %collective-permute-start.23 = (bf16[224,512]{1,0:T(8,128)(2,1)S(1)}, bf16[224,512]{1,0:T(8,128)(2,1)S(1)}, u32[]{:S(2)}, u32[]{:S(2)}) collective-permute-start(bf16[224,512]{1,0:T(8,128)(2,1)S(1)} %get-tuple-element.82), channel_id=1, source_target_pairs={{0,3},{1,0},{2,1},{3,2},{4,7},{5,4},{6,5},{7,6},{8,11},{9,8},{10,9... | collective-permute-start | bytes 688136 | tf_op jit(solution)/shard_map/ppermute | solution.py:41
  74.1 1.3 %collective-permute-start.20 = (bf16[64,512]{1,0:T(8,128)(2,1)S(1)}, bf16[64,512]{1,0:T(8,128)(2,1)S(1)}, u32[]{:S(2)}, u32[]{:S(2)}) collective-permute-start(bf16[64,512]{1,0:T(8,128)(2,1)S(1)} %get-tuple-element.78.refs_5_), channel_id=1, source_target_pairs={{0,8},{8,0},{16,24},{24,16},{32,40},{40,32},{48,56},{56,48},{64,72... | collective-permute-start | bytes 196616 | tf_op jit(solution)/shard_map/ppermute | solution.py:49
  (2 other events, 20.2 us)

commit v4 on v3

--- a/solution.py
+++ b/solution.py
@@ -16,7 +16,7 @@
 N_REP = 32
 HALF = SLAB // 2
 PART = HALF // 2
-LOWER = 288
+LOWER = 320
 UPPER = SLAB - LOWER
 SOME = LOWER // 2
 ORDER = (6, 2, 3, 5, 7, 4, 1, 0)

time: 83.7 us -> 82.3 us (0.983)
  starting transfers between devices: 37.3 us -> 36.4 us
    ppermute x6, starting transfers between devices: 5.58 us -> 7.22 us  [move_z(): return lax.ppermute(value, 'fsdp', [(i, (i + 4) % 8) for i in range(8)])]
    ppermute x2, starting transfers between devices: 7.63 us -> 6.34 us  [swap_z(): return lax.ppermute(value, 'rep', pairs)]
    ppermute x12, starting transfers between devices: 19.7 us -> 18.4 us  [move_y(): return lax.ppermute(value, 'fsdp', pairs)]
  transfers between devices with their start and end apart: 24 -> 24, of which waited for: 14 -> 12; matrix products, arithmetic and copies ran while one was open for 0% -> 0% of each run, Pallas kernels for 19% -> 19%
where the time goes in v4:
time: 82.3 us; the launch traced here: 82.2 us
  starting transfers between devices  36.4 us (44%)
  waiting for transfers between devices  22.9 us (28%)
  Pallas kernels  21.1 us (26%)
  between operations  0.97 us (1%)
    pallas_call x17, Pallas kernels, local_call(): pl.pallas_call(run, out_shape=outs, in_specs=[SMEM] * len(scalars) + [VME...  21.1 us
    ppermute x12, starting transfers between devices, move_y(): return lax.ppermute(value, 'fsdp', pairs)  18.4 us
    ppermute x12, waiting for transfers between devices, move_y(): return lax.ppermute(value, 'fsdp', pairs)  8.88 us
    ppermute x2, waiting for transfers between devices, swap_z(): return lax.ppermute(value, 'rep', pairs)  8.49 us
    ppermute x6, starting transfers between devices, move_z(): return lax.ppermute(value, 'fsdp', [(i, (i + 4) % 8) for i in range(8)])  7.22 us
    ppermute x2, starting transfers between devices, swap_z(): return lax.ppermute(value, 'rep', pairs)  6.34 us
    ppermute x2, starting transfers between devices, swap_x(): return lax.ppermute(value, 'rep', pairs)  4.34 us
    ppermute x2, waiting for transfers between devices, swap_x(): return lax.ppermute(value, 'rep', pairs)  2.78 us
  transfers between devices with their start and end apart: 24, of which 12 were waited for; matrix products, arithmetic and copies ran while one was open for 0% of the time, Pallas kernels for 19%

profile of v4, /device:TPU:24, one launch (start us, length us, event | category | flops | bytes accessed | tf_op | source)
XLA Modules:
  0.0 82.2 jit_solution(5357689833893791544)
XLA Ops:
  1.9 2.0 %collective-permute-start = (bf16[256,512]{1,0:T(8,128)(2,1)S(1)}, bf16[256,512]{1,0:T(8,128)(2,1)S(1)}, u32[]{:S(2)}, u32[]{:S(2)}) collective-permute-start(bf16[256,512]{1,0:T(8,128)(2,1)S(1)} %get-tuple-element.48.refs_0_), channel_id=1, source_target_pairs={{0,1},{1,2},{2,3},{3,0},{4,5},{5,6},{6,7},{7,4},{8,9},{9,10},{10,1... | collective-permute-start | bytes 786440 | tf_op jit(solution)/shard_map/ppermute | solution.py:41
  4.1 1.8 %collective-permute-start.7 = (bf16[256,512]{1,0:T(8,128)(2,1)S(1)}, bf16[256,512]{1,0:T(8,128)(2,1)S(1)}, u32[]{:S(2)}, u32[]{:S(2)}) collective-permute-start(bf16[256,512]{1,0:T(8,128)(2,1)S(1)} %get-tuple-element.48.refs_0_), channel_id=1, source_target_pairs={{0,3},{1,0},{2,1},{3,2},{4,7},{5,4},{6,5},{7,6},{8,11},{9,8},{10,9... | collective-permute-start | bytes 786440 | tf_op jit(solution)/shard_map/ppermute | solution.py:41
  6.6 1.6 %shard_map.128 = (bf16[64,512]{1,0:T(8,128)(2,1)S(1)}, bf16[64,512]{1,0:T(8,128)(2,1)S(1)}) custom-call(s32[2]{0:T(128)S(1)} %pad_add_fusion.refs_0_, s32[4]{0:T(128)S(1)} %copy-done, f32[512,512]{1,0:T(8,128)} %bitcast.7, f32[512,512]{1,0:T(8,128)} %refs_1_.6, bf16[512,512]{1,0:T(8,128)(2,1)S(1)} %get-tuple-element.49.refs_4_.refs_1_.refs_2_), custom_call_target="tpu_custom_call" | custom-call | flops 1024 | bytes 1024 | tf_op jit(solution)/shard_map/pallas_call | solution.py:109
  15.8 2.8 %collective-permute-done.5.refs_1_ = bf16[64,512]{1,0:T(8,128)(2,1)S(1)} collective-permute-done((bf16[64,512]{1,0:T(8,128)(2,1)S(1)}, bf16[64,512]{1,0:T(8,128)(2,1)S(1)}, u32[]{:S(2)}, u32[]{:S(2)}) %collective-permute-start.5) | collective-permute-done | bytes 65568 | tf_op jit(solution)/shard_map/ppermute | solution.py:57
  18.6 2.8 %collective-permute-start.6 = (bf16[64,512]{1,0:T(8,128)(2,1)S(1)}, bf16[64,512]{1,0:T(8,128)(2,1)S(1)}, u32[]{:S(2)}, u32[]{:S(2)}) collective-permute-start(bf16[64,512]{1,0:T(8,128)(2,1)S(1)} %shard_map.130.refs_3_), channel_id=1, source_target_pairs={{0,48},{8,56},{16,32},{24,40},{32,16},{40,24},{48,0},{56,8},{64,11... | collective-permute-start | bytes 196616 | tf_op jit(solution)/shard_map/ppermute | solution.py:57
  21.5 3.2 %shard_map.131 = (bf16[8,512,512]{2,1,0:T(8,128)(2,1)S(1)}, bf16[8,512,512]{2,1,0:T(8,128)(2,1)S(1)}, bf16[512,512]{1,0:T(8,128)(2,1)S(1)}) custom-call(s32[2]{0:T(128)S(1)} %pad_add_fusion.refs_0_, bf16[512,4096]{1,0:T(8,128)(2,1)} %refs_1_.5, bf16[512,512]{1,0:T(8,128)(2,1)} %refs_2_.2, bf16[64,512]{1,0:T(8,128)(2,1)S(1)} %get-tuple-element.54.refs_0_.refs_3_), custom_call_target="tpu_custom_call" | custom-call | flops 1024 | bytes 1024 | tf_op jit(solution)/shard_map/pallas_call | solution.py:109
  26.6 3.0 %collective-permute-start.9 = (bf16[384,512]{1,0:T(8,128)(2,1)S(1)}, bf16[384,512]{1,0:T(8,128)(2,1)S(1)}, u32[]{:S(2)}, u32[]{:S(2)}) collective-permute-start(bf16[384,512]{1,0:T(8,128)(2,1)S(1)} %get-tuple-element.62), channel_id=1, source_target_pairs={{0,1},{1,2},{2,3},{3,0},{4,5},{5,6},{6,7},{7,4},{8,9},{9,10},{10,1... | collective-permute-start | bytes 1179656 | tf_op jit(solution)/shard_map/ppermute | solution.py:41
  29.5 1.8 %collective-permute-start.11 = (bf16[256,512]{1,0:T(8,128)(2,1)S(1)}, bf16[256,512]{1,0:T(8,128)(2,1)S(1)}, u32[]{:S(2)}, u32[]{:S(2)}) collective-permute-start(bf16[256,512]{1,0:T(8,128)(2,1)S(1)} %get-tuple-element.56.refs_6_), channel_id=1, source_target_pairs={{0,4},{1,5},{2,6},{3,7},{4,0},{5,1},{6,2},{7,3},{8,12},{9,13},{10,... | collective-permute-start | bytes 786440 | tf_op jit(solution)/shard_map/ppermute | solution.py:45
  31.4 3.6 %shard_map.133 = (f32[128,512]{1,0:T(8,128)S(1)}, f32[512,512]{1,0:T(8,128)S(1)}, f32[512,512]{1,0:T(8,128)S(1)}, f32[512,512]{1,0:T(8,128)}, f32[512,512]{1,0:T(8,128)}) custom-call(s32[4]{0:T(128)S(1)} %copy-done.1, f32[512,512]{1,0:T(8,128)} %refs_1_.6, f32[512,512]{1,0:T(8,128)} %refs_2_.3, f32[128,512]{1,0:T(8,128)} %refs_3_.3, f32[512,512]{1,0:T(8,128)} %bitcast.8, ...), custom_call_target="tpu_custom_call" | custom-call | flops 1024 | bytes 1024 | tf_op jit(solution)/shard_map/pallas_call | solution.py:109
  35.0 1.8 %shard_map.135.refs_2_ = f32[512,512]{1,0:T(8,128)S(1)} custom-call(bf16[8,512,512]{2,1,0:T(8,128)(2,1)S(1)} %get-tuple-element.61.refs_0_, bf16[512,512]{1,0:T(8,128)(2,1)S(1)} %get-tuple-element.49.refs_4_.refs_1_.refs_2_, bf16[256,512]{1,0:T(8,128)(2,1)S(1)} %collective-permute-done.7.refs_2_.refs_3_, ...), custom_call_target="tpu_custom_call" | custom-call | flops 1024 | bytes 1024 | tf_op jit(solution)/shard_map/pallas_call | solution.py:109
  36.9 1.6 %shard_map.136 = (bf16[512,512]{1,0:T(8,128)(2,1)S(1)}, bf16[480,512]{1,0:T(8,128)(2,1)S(1)}, bf16[480,512]{1,0:T(8,128)(2,1)S(1)}, bf16[192,512]{1,0:T(8,128)(2...) custom-call(bf16[8,512,512]{2,1,0:T(8,128)(2,1)S(1)} %get-tuple-element.61.refs_0_, ...), custom_call_target="tpu_custom_call" | custom-call | flops 1024 | bytes 1024 | tf_op jit(solution)/shard_map/pallas_call | solution.py:109
  38.5 3.2 %collective-permute-start.12 = (bf16[480,512]{1,0:T(8,128)(2,1)S(1)}, bf16[480,512]{1,0:T(8,128)(2,1)S(1)}, u32[]{:S(2)}, u32[]{:S(2)}) collective-permute-start(bf16[480,512]{1,0:T(8,128)(2,1)S(1)} %get-tuple-element.69), channel_id=1, source_target_pairs={{0,1},{1,2},{2,3},{3,0},{4,5},{5,6},{6,7},{7,4},{8,9},{9,10},{10,1... | collective-permute-start | bytes 1474568 | tf_op jit(solution)/shard_map/ppermute | solution.py:41
  41.7 1.9 %collective-permute-start.15 = (bf16[192,512]{1,0:T(8,128)(2,1)S(1)}, bf16[192,512]{1,0:T(8,128)(2,1)S(1)}, u32[]{:S(2)}, u32[]{:S(2)}) collective-permute-start(bf16[192,512]{1,0:T(8,128)(2,1)S(1)} %get-tuple-element.73), channel_id=1, source_target_pairs={{0,4},{1,5},{2,6},{3,7},{4,0},{5,1},{6,2},{7,3},{8,12},{9,13},{10,... | collective-permute-start | bytes 589832 | tf_op jit(solution)/shard_map/ppermute | solution.py:45
  43.7 2.1 %collective-permute-start.17 = (bf16[64,512]{1,0:T(8,128)(2,1)S(1)}, bf16[64,512]{1,0:T(8,128)(2,1)S(1)}, u32[]{:S(2)}, u32[]{:S(2)}) collective-permute-start(bf16[64,512]{1,0:T(8,128)(2,1)S(1)} %get-tuple-element.75.refs_1_), channel_id=1, source_target_pairs={{0,64},{8,72},{16,80},{24,88},{32,96},{40,104},{48,112},{56,120},{... | collective-permute-start | bytes 196616 | tf_op jit(solution)/shard_map/ppermute | solution.py:65
  45.7 1.5 %shard_map.137 = (bf16[320,512]{1,0:T(8,128)(2,1)S(1)}, bf16[320,512]{1,0:T(8,128)(2,1)S(1)}, bf16[320,512]{1,0:T(8,128)(2,1)S(1)}, bf16[576,512]{1,0:T(8,128)(2...) custom-call(bf16[8,512,512]{2,1,0:T(8,128)(2,1)S(1)} %get-tuple-element.60.refs_1_.refs_0_, ...), custom_call_target="tpu_custom_call" | custom-call | flops 1024 | bytes 1024 | tf_op jit(solution)/shard_map/pallas_call | solution.py:109
  47.2 2.8 %collective-permute-done.12.refs_2_ = bf16[480,512]{1,0:T(8,128)(2,1)S(1)} collective-permute-done((bf16[480,512]{1,0:T(8,128)(2,1)S(1)}, bf16[480,512]{1,0:T(8,128)(2,1)S(1)}, u32[]{:S(2)}, u32[]{:S(2)}) %collective-permute-start.12) | collective-permute-done | bytes 491552 | tf_op jit(solution)/shard_map/ppermute | solution.py:41
  50.2 3.8 %collective-permute-start.13 = (bf16[640,512]{1,0:T(8,128)(2,1)S(1)}, bf16[640,512]{1,0:T(8,128)(2,1)S(1)}, u32[]{:S(2)}, u32[]{:S(2)}) collective-permute-start(bf16[640,512]{1,0:T(8,128)(2,1)S(1)} %shard_map.138.refs_4_), channel_id=1, source_target_pairs={{0,1},{1,2},{2,3},{3,0},{4,5},{5,6},{6,7},{7,4},{8,9},{9,10},{10,1... | collective-permute-start | bytes 1966088 | tf_op jit(solution)/shard_map/ppermute | solution.py:41
  54.0 1.8 %collective-permute-start.18 = (bf16[576,512]{1,0:T(8,128)(2,1)S(1)}, bf16[576,512]{1,0:T(8,128)(2,1)S(1)}, u32[]{:S(2)}, u32[]{:S(2)}) collective-permute-start(bf16[576,512]{1,0:T(8,128)(2,1)S(1)} %get-tuple-element.76), channel_id=1, source_target_pairs={{0,4},{1,5},{2,6},{3,7},{4,0},{5,1},{6,2},{7,3},{8,12},{9,13},{10,... | collective-permute-start | bytes 1769480 | tf_op jit(solution)/shard_map/ppermute | solution.py:45
  56.0 4.3 %collective-permute-start.19 = (bf16[64,512]{1,0:T(8,128)(2,1)S(1)}, bf16[64,512]{1,0:T(8,128)(2,1)S(1)}, u32[]{:S(2)}, u32[]{:S(2)}) collective-permute-start(bf16[64,512]{1,0:T(8,128)(2,1)S(1)} %get-tuple-element.77.refs_6_), channel_id=1, source_target_pairs={{0,192},{8,200},{16,208},{24,216},{32,224},{40,232},{48,240},{56,2... | collective-permute-start | bytes 196616 | tf_op jit(solution)/shard_map/ppermute | solution.py:65
  60.3 3.8 %shard_map.141.refs_8_ = bf16[512,4096]{1,0:T(8,128)(2,1)} custom-call(s32[2]{0:T(128)S(1)} %pad_add_fusion.refs_0_, bf16[512,512]{1,0:T(8,128)(2,1)S(1)} %get-tuple-element.64.refs_1_, bf16[512,512]{1,0:T(8,128)(2,1)S(1)} %get-tuple-element.49.refs_4_.refs_1_.refs_2_, bf16[256,512]{1,0:T(8,128)(2,1)S(1)} %collective-permute-done.7.refs_2_.refs_3_, ...), custom_call_target="tpu_custom_call" | custom-call | flops 1024 | bytes 1024 | tf_op jit(solution)/shard_map/pallas_call | solution.py:109
  64.1 8.5 %collective-permute-done.19.refs_7_ = bf16[64,512]{1,0:T(8,128)(2,1)S(1)} collective-permute-done((bf16[64,512]{1,0:T(8,128)(2,1)S(1)}, bf16[64,512]{1,0:T(8,128)(2,1)S(1)}, u32[]{:S(2)}, u32[]{:S(2)}) %collective-permute-start.19) | collective-permute-done | bytes 65568 | tf_op jit(solution)/shard_map/ppermute | solution.py:65
  73.0 2.0 %collective-permute-start.23 = (bf16[192,512]{1,0:T(8,128)(2,1)S(1)}, bf16[192,512]{1,0:T(8,128)(2,1)S(1)}, u32[]{:S(2)}, u32[]{:S(2)}) collective-permute-start(bf16[192,512]{1,0:T(8,128)(2,1)S(1)} %get-tuple-element.82), channel_id=1, source_target_pairs={{0,3},{1,0},{2,1},{3,2},{4,7},{5,4},{6,5},{7,6},{8,11},{9,8},{10,9... | collective-permute-start | bytes 589832 | tf_op jit(solution)/shard_map/ppermute | solution.py:41
  76.3 2.4 %collective-permute-done.22.refs_12_ = bf16[192,512]{1,0:T(8,128)(2,1)S(1)} collective-permute-done((bf16[192,512]{1,0:T(8,128)(2,1)S(1)}, bf16[192,512]{1,0:T(8,128)(2,1)S(1)}, u32[]{:S(2)}, u32[]{:S(2)}) %collective-permute-start.22) | collective-permute-done | bytes 196640 | tf_op jit(solution)/shard_map/ppermute | solution.py:41
  80.0 2.0 %shard_map.143 = (f32[512,512]{1,0:T(8,128)}, f32[512,512]{1,0:T(8,128)}, f32[128,512]{1,0:T(8,128)}) custom-call(s32[2]{0:T(128)S(1)} %pad_add_fusion.refs_0_, s32[4]{0:T(128)S(1)} %copy-done.1, f32[128,512]{1,0:T(8,128)S(1)} %get-tuple-element.57.refs_8_.refs_2_, f32[512,512]{1,0:T(8,128)S(1)} %get-tuple-element.58.refs_3_, ...), custom_call_target="tpu_custom_call" | custom-call | flops 1024 | bytes 1024 | tf_op jit(solution)/shard_map/pallas_call | solution.py:109
  (46 shorter events, 15.0 us)
Async XLA Ops:
  1.9 8.1 %collective-permute-start = (bf16[256,512]{1,0:T(8,128)(2,1)S(1)}, bf16[256,512]{1,0:T(8,128)(2,1)S(1)}, u32[]{:S(2)}, u32[]{:S(2)}) collective-permute-start(bf16[256,512]{1,0:T(8,128)(2,1)S(1)} %get-tuple-element.48.refs_0_), channel_id=1, source_target_pairs={{0,1},{1,2},{2,3},{3,0},{4,5},{5,6},{6,7},{7,4},{8,9},{9,10},{10,1... | collective-permute-start | bytes 786440 | tf_op jit(solution)/shard_map/ppermute | solution.py:41
  3.9 6.4 %collective-permute-start.1 = (bf16[256,512]{1,0:T(8,128)(2,1)S(1)}, bf16[256,512]{1,0:T(8,128)(2,1)S(1)}, u32[]{:S(2)}, u32[]{:S(2)}) collective-permute-start(bf16[256,512]{1,0:T(8,128)(2,1)S(1)} %get-tuple-element.47.refs_0_), channel_id=1, source_target_pairs={{0,4},{1,5},{2,6},{3,7},{4,0},{5,1},{6,2},{7,3},{8,12},{9,13},{10,... | collective-permute-start | bytes 786440 | tf_op jit(solution)/shard_map/ppermute | solution.py:45
  4.1 8.9 %collective-permute-start.7 = (bf16[256,512]{1,0:T(8,128)(2,1)S(1)}, bf16[256,512]{1,0:T(8,128)(2,1)S(1)}, u32[]{:S(2)}, u32[]{:S(2)}) collective-permute-start(bf16[256,512]{1,0:T(8,128)(2,1)S(1)} %get-tuple-element.48.refs_0_), channel_id=1, source_target_pairs={{0,3},{1,0},{2,1},{3,2},{4,7},{5,4},{6,5},{7,6},{8,11},{9,8},{10,9... | collective-permute-start | bytes 786440 | tf_op jit(solution)/shard_map/ppermute | solution.py:41
  8.3 1.3 %collective-permute-start.2 = (bf16[64,512]{1,0:T(8,128)(2,1)S(1)}, bf16[64,512]{1,0:T(8,128)(2,1)S(1)}, u32[]{:S(2)}, u32[]{:S(2)}) collective-permute-start(bf16[64,512]{1,0:T(8,128)(2,1)S(1)} %get-tuple-element.51), channel_id=1, source_target_pairs={{0,8},{8,0},{16,24},{24,16},{32,40},{40,32},{48,56},{56,48},{64,72... | collective-permute-start | bytes 196616 | tf_op jit(solution)/shard_map/ppermute | solution.py:49
  10.4 14.3 %collective-permute-start.3 = (bf16[512,512]{1,0:T(8,128)(2,1)S(1)}, bf16[512,512]{1,0:T(8,128)(2,1)S(1)}, u32[]{:S(2)}, u32[]{:S(2)}) collective-permute-start(bf16[512,512]{1,0:T(8,128)(2,1)S(1)} %get-tuple-element.52), channel_id=1, source_target_pairs={{0,1},{1,2},{2,3},{3,0},{4,5},{5,6},{6,7},{7,4},{8,9},{9,10},{10,1... | collective-permute-start | bytes 1572872 | tf_op jit(solution)/shard_map/ppermute | solution.py:41
  11.9 14.3 %collective-permute-start.4 = (bf16[512,512]{1,0:T(8,128)(2,1)S(1)}, bf16[512,512]{1,0:T(8,128)(2,1)S(1)}, u32[]{:S(2)}, u32[]{:S(2)}) collective-permute-start(bf16[512,512]{1,0:T(8,128)(2,1)S(1)} %get-tuple-element.53), channel_id=1, source_target_pairs={{0,3},{1,0},{2,1},{3,2},{4,7},{5,4},{6,5},{7,6},{8,11},{9,8},{10,9... | collective-permute-start | bytes 1572872 | tf_op jit(solution)/shard_map/ppermute | solution.py:41
  13.0 22.0 %collective-permute-start.8 = (bf16[768,512]{1,0:T(8,128)(2,1)S(1)}, bf16[768,512]{1,0:T(8,128)(2,1)S(1)}, u32[]{:S(2)}, u32[]{:S(2)}) collective-permute-start(bf16[768,512]{1,0:T(8,128)(2,1)S(1)} %shard_map.134), channel_id=1, source_target_pairs={{0,4},{1,5},{2,6},{3,7},{4,0},{5,1},{6,2},{7,3},{8,12},{9,13},{10,... | collective-permute-start | bytes 2359304 | tf_op jit(solution)/shard_map/ppermute | solution.py:45
  14.4 4.3 %collective-permute-start.5 = (bf16[64,512]{1,0:T(8,128)(2,1)S(1)}, bf16[64,512]{1,0:T(8,128)(2,1)S(1)}, u32[]{:S(2)}, u32[]{:S(2)}) collective-permute-start(bf16[64,512]{1,0:T(8,128)(2,1)S(1)} %get-tuple-element.54.refs_0_.refs_3_), channel_id=1, source_target_pairs={{0,16},{8,24},{16,0},{24,8},{32,48},{40,56},{48,32},{56,40},{64,80... | collective-permute-start | bytes 196616 | tf_op jit(solution)/shard_map/ppermute | solution.py:57
  18.6 6.1 %collective-permute-start.6 = (bf16[64,512]{1,0:T(8,128)(2,1)S(1)}, bf16[64,512]{1,0:T(8,128)(2,1)S(1)}, u32[]{:S(2)}, u32[]{:S(2)}) collective-permute-start(bf16[64,512]{1,0:T(8,128)(2,1)S(1)} %shard_map.130.refs_3_), channel_id=1, source_target_pairs={{0,48},{8,56},{16,32},{24,40},{32,16},{40,24},{48,0},{56,8},{64,11... | collective-permute-start | bytes 196616 | tf_op jit(solution)/shard_map/ppermute | solution.py:57
  26.2 10.6 %collective-permute-start.10 = (bf16[384,512]{1,0:T(8,128)(2,1)S(1)}, bf16[384,512]{1,0:T(8,128)(2,1)S(1)}, u32[]{:S(2)}, u32[]{:S(2)}) collective-permute-start(bf16[384,512]{1,0:T(8,128)(2,1)S(1)} %get-tuple-element.63), channel_id=1, source_target_pairs={{0,3},{1,0},{2,1},{3,2},{4,7},{5,4},{6,5},{7,6},{8,11},{9,8},{10,9... | collective-permute-start | bytes 1179656 | tf_op jit(solution)/shard_map/ppermute | solution.py:41
  26.6 10.3 %collective-permute-start.9 = (bf16[384,512]{1,0:T(8,128)(2,1)S(1)}, bf16[384,512]{1,0:T(8,128)(2,1)S(1)}, u32[]{:S(2)}, u32[]{:S(2)}) collective-permute-start(bf16[384,512]{1,0:T(8,128)(2,1)S(1)} %get-tuple-element.62), channel_id=1, source_target_pairs={{0,1},{1,2},{2,3},{3,0},{4,5},{5,6},{6,7},{7,4},{8,9},{9,10},{10,1... | collective-permute-start | bytes 1179656 | tf_op jit(solution)/shard_map/ppermute | solution.py:41
  29.5 7.2 %collective-permute-start.11 = (bf16[256,512]{1,0:T(8,128)(2,1)S(1)}, bf16[256,512]{1,0:T(8,128)(2,1)S(1)}, u32[]{:S(2)}, u32[]{:S(2)}) collective-permute-start(bf16[256,512]{1,0:T(8,128)(2,1)S(1)} %get-tuple-element.56.refs_6_), channel_id=1, source_target_pairs={{0,4},{1,5},{2,6},{3,7},{4,0},{5,1},{6,2},{7,3},{8,12},{9,13},{10,... | collective-permute-start | bytes 786440 | tf_op jit(solution)/shard_map/ppermute | solution.py:45
  38.5 11.6 %collective-permute-start.12 = (bf16[480,512]{1,0:T(8,128)(2,1)S(1)}, bf16[480,512]{1,0:T(8,128)(2,1)S(1)}, u32[]{:S(2)}, u32[]{:S(2)}) collective-permute-start(bf16[480,512]{1,0:T(8,128)(2,1)S(1)} %get-tuple-element.69), channel_id=1, source_target_pairs={{0,1},{1,2},{2,3},{3,0},{4,5},{5,6},{6,7},{7,4},{8,9},{9,10},{10,1... | collective-permute-start | bytes 1474568 | tf_op jit(solution)/shard_map/ppermute | solution.py:41
  41.7 14.1 %collective-permute-start.14 = (bf16[480,512]{1,0:T(8,128)(2,1)S(1)}, bf16[480,512]{1,0:T(8,128)(2,1)S(1)}, u32[]{:S(2)}, u32[]{:S(2)}) collective-permute-start(bf16[480,512]{1,0:T(8,128)(2,1)S(1)} %get-tuple-element.72), channel_id=1, source_target_pairs={{0,3},{1,0},{2,1},{3,2},{4,7},{5,4},{6,5},{7,6},{8,11},{9,8},{10,9... | collective-permute-start | bytes 1474568 | tf_op jit(solution)/shard_map/ppermute | solution.py:41
  41.7 14.1 %collective-permute-start.15 = (bf16[192,512]{1,0:T(8,128)(2,1)S(1)}, bf16[192,512]{1,0:T(8,128)(2,1)S(1)}, u32[]{:S(2)}, u32[]{:S(2)}) collective-permute-start(bf16[192,512]{1,0:T(8,128)(2,1)S(1)} %get-tuple-element.73), channel_id=1, source_target_pairs={{0,4},{1,5},{2,6},{3,7},{4,0},{5,1},{6,2},{7,3},{8,12},{9,13},{10,... | collective-permute-start | bytes 589832 | tf_op jit(solution)/shard_map/ppermute | solution.py:45
  43.7 10.3 %collective-permute-start.17 = (bf16[64,512]{1,0:T(8,128)(2,1)S(1)}, bf16[64,512]{1,0:T(8,128)(2,1)S(1)}, u32[]{:S(2)}, u32[]{:S(2)}) collective-permute-start(bf16[64,512]{1,0:T(8,128)(2,1)S(1)} %get-tuple-element.75.refs_1_), channel_id=1, source_target_pairs={{0,64},{8,72},{16,80},{24,88},{32,96},{40,104},{48,112},{56,120},{... | collective-permute-start | bytes 196616 | tf_op jit(solution)/shard_map/ppermute | solution.py:65
  50.2 22.4 %collective-permute-start.13 = (bf16[640,512]{1,0:T(8,128)(2,1)S(1)}, bf16[640,512]{1,0:T(8,128)(2,1)S(1)}, u32[]{:S(2)}, u32[]{:S(2)}) collective-permute-start(bf16[640,512]{1,0:T(8,128)(2,1)S(1)} %shard_map.138.refs_4_), channel_id=1, source_target_pairs={{0,1},{1,2},{2,3},{3,0},{4,5},{5,6},{6,7},{7,4},{8,9},{9,10},{10,1... | collective-permute-start | bytes 1966088 | tf_op jit(solution)/shard_map/ppermute | solution.py:41
  54.0 18.6 %collective-permute-start.18 = (bf16[576,512]{1,0:T(8,128)(2,1)S(1)}, bf16[576,512]{1,0:T(8,128)(2,1)S(1)}, u32[]{:S(2)}, u32[]{:S(2)}) collective-permute-start(bf16[576,512]{1,0:T(8,128)(2,1)S(1)} %get-tuple-element.76), channel_id=1, source_target_pairs={{0,4},{1,5},{2,6},{3,7},{4,0},{5,1},{6,2},{7,3},{8,12},{9,13},{10,... | collective-permute-start | bytes 1769480 | tf_op jit(solution)/shard_map/ppermute | solution.py:45
  55.9 16.7 %collective-permute-start.16 = (bf16[512,512]{1,0:T(8,128)(2,1)S(1)}, bf16[512,512]{1,0:T(8,128)(2,1)S(1)}, u32[]{:S(2)}, u32[]{:S(2)}) collective-permute-start(bf16[512,512]{1,0:T(8,128)(2,1)S(1)} %shard_map.139.refs_12_), channel_id=1, source_target_pairs={{0,3},{1,0},{2,1},{3,2},{4,7},{5,4},{6,5},{7,6},{8,11},{9,8},{10,9... | collective-permute-start | bytes 1572872 | tf_op jit(solution)/shard_map/ppermute | solution.py:41
  56.0 16.6 %collective-permute-start.19 = (bf16[64,512]{1,0:T(8,128)(2,1)S(1)}, bf16[64,512]{1,0:T(8,128)(2,1)S(1)}, u32[]{:S(2)}, u32[]{:S(2)}) collective-permute-start(bf16[64,512]{1,0:T(8,128)(2,1)S(1)} %get-tuple-element.77.refs_6_), channel_id=1, source_target_pairs={{0,192},{8,200},{16,208},{24,216},{32,224},{40,232},{48,240},{56,2... | collective-permute-start | bytes 196616 | tf_op jit(solution)/shard_map/ppermute | solution.py:65
  72.8 7.2 %collective-permute-start.21 = (bf16[320,512]{1,0:T(8,128)(2,1)S(1)}, bf16[320,512]{1,0:T(8,128)(2,1)S(1)}, u32[]{:S(2)}, u32[]{:S(2)}) collective-permute-start(bf16[320,512]{1,0:T(8,128)(2,1)S(1)} %get-tuple-element.80), channel_id=1, source_target_pairs={{0,4},{1,5},{2,6},{3,7},{4,0},{5,1},{6,2},{7,3},{8,12},{9,13},{10,... | collective-permute-start | bytes 983048 | tf_op jit(solution)/shard_map/ppermute | solution.py:45
  72.9 5.7 %collective-permute-start.22 = (bf16[192,512]{1,0:T(8,128)(2,1)S(1)}, bf16[192,512]{1,0:T(8,128)(2,1)S(1)}, u32[]{:S(2)}, u32[]{:S(2)}) collective-permute-start(bf16[192,512]{1,0:T(8,128)(2,1)S(1)} %get-tuple-element.81), channel_id=1, source_target_pairs={{0,1},{1,2},{2,3},{3,0},{4,5},{5,6},{6,7},{7,4},{8,9},{9,10},{10,1... | collective-permute-start | bytes 589832 | tf_op jit(solution)/shard_map/ppermute | solution.py:41
  73.0 7.0 %collective-permute-start.23 = (bf16[192,512]{1,0:T(8,128)(2,1)S(1)}, bf16[192,512]{1,0:T(8,128)(2,1)S(1)}, u32[]{:S(2)}, u32[]{:S(2)}) collective-permute-start(bf16[192,512]{1,0:T(8,128)(2,1)S(1)} %get-tuple-element.82), channel_id=1, source_target_pairs={{0,3},{1,0},{2,1},{3,2},{4,7},{5,4},{6,5},{7,6},{8,11},{9,8},{10,9... | collective-permute-start | bytes 589832 | tf_op jit(solution)/shard_map/ppermute | solution.py:41
  75.0 1.3 %collective-permute-start.20 = (bf16[64,512]{1,0:T(8,128)(2,1)S(1)}, bf16[64,512]{1,0:T(8,128)(2,1)S(1)}, u32[]{:S(2)}, u32[]{:S(2)}) collective-permute-start(bf16[64,512]{1,0:T(8,128)(2,1)S(1)} %get-tuple-element.78.refs_5_), channel_id=1, source_target_pairs={{0,8},{8,0},{16,24},{24,16},{32,40},{40,32},{48,56},{56,48},{64,72... | collective-permute-start | bytes 196616 | tf_op jit(solution)/shard_map/ppermute | solution.py:49
  (2 other events, 20.2 us)
